TPU v7x, 512 devices: a whole 4x8x8 slice. The times are simulated.
512 devices in a mesh: gy: 16 (over y, core), gz: 32 (over x, z).
Axes of the slice: x: 4, y: 8, z: 8, core: 2. Of those that a mesh axis runs over, the one named last changes fastest.
Arguments:
- force: float32 [3, 512, 256, 128], P(None, 'gy', 'gz'), may hold values from -6 to 6
- density: float32 [512, 256, 128], P('gy', 'gz'), may hold values from 0.2 to 1
- solid_blocks: int32 [64, 32, 16], P('gy', 'gz'), may hold values from 0 to 1, as said below
- fixed_nodes: int32 [512, 256, 128], P('gy', 'gz'), may hold values 0 or 1
- filter_gain: float32 [256], replicated, may hold values from 0.05 to 1
Outputs:
- displacement: float32 [3, 512, 256, 128], P(None, 'gy', 'gz')
- filtered: float32 [512, 256, 128], P(('gy', 'gz'))
Inputs may be any that keep to these rules, and one draw needn't show every extreme that they name: `solid_blocks`: 1 marks a solid block, 0 a void one; the last block along y is solid everywhere.
All inputs are finite; a program needn't handle non-finite values. No bound on the sum of `fixed_nodes` on one device may be relied on, other than what follows from the above.
Results may differ from a plain program's by a relative error of at most 0.0003.
Values sent between devices are 32-bit elements; how exact they have to be, the bound alone decides.
A program may use at most 64 MiB of HBM per device.

v0:
```python
import jax
import jax.numpy as jnp
import numpy as np
from jax import lax
from jax.sharding import PartitionSpec as P

ITERS = 3


MIN_MODULUS = 0.1
DIAG_FLOOR = 0.5
CORNERS = [(a, b, c) for a in (0, 1) for b in (0, 1) for c in (0, 1)]
HIGHEST = lax.Precision.HIGHEST


def passed_along(value, axis, steps):
    count = lax.axis_size(axis)
    first, last = (max(0, -steps), min(count, count - steps))
    return lax.ppermute(value, axis, [(source, source + steps) for source in range(first, last)])


def with_halo(x, sides, width):
    for axis, dim in sides:
        count, length = (lax.axis_size(axis), x.shape[dim])
        up = [(i, (i + 1) % count) for i in range(count - 1)]
        down = [(j, i) for i, j in up]
        last = lax.slice_in_dim(x, length - width, length, axis=dim)
        first = lax.slice_in_dim(x, 0, width, axis=dim)
        before = lax.ppermute(last, axis, up)
        after = lax.ppermute(first, axis, down)
        x = jnp.concatenate([before, x, after], axis=dim)
    return x


def element_matrix():
    poisson = 0.3
    lame_first = poisson / ((1.0 + poisson) * (1.0 - 2.0 * poisson))
    shear_modulus = 1.0 / (2.0 * (1.0 + poisson))
    elastic = np.zeros((6, 6))
    elastic[:3, :3] = lame_first
    for axis in range(3):
        elastic[axis, axis] = lame_first + 2.0 * shear_modulus
        elastic[3 + axis, 3 + axis] = shear_modulus
    gauss_points = [0.5 - 0.5 / np.sqrt(3.0), 0.5 + 0.5 / np.sqrt(3.0)]
    stiffness = np.zeros((24, 24))
    for first in gauss_points:
        for second in gauss_points:
            for third in gauss_points:
                location = (first, second, third)
                strain = np.zeros((6, 24))
                for corner, corner_bits in enumerate(CORNERS):
                    gradient = []
                    for axis in range(3):
                        amount = 1.0
                        for other in range(3):
                            if other == axis:
                                amount *= 1.0 if corner_bits[other] else -1.0
                            else:
                                amount *= (
                                    location[other] if corner_bits[other] else 1.0 - location[other]
                                )
                        gradient.append(amount)
                    column = 3 * corner
                    strain[0, column] = gradient[0]
                    strain[1, column + 1] = gradient[1]
                    strain[2, column + 2] = gradient[2]
                    strain[3, column] = gradient[1]
                    strain[3, column + 1] = gradient[0]
                    strain[4, column + 1] = gradient[2]
                    strain[4, column + 2] = gradient[1]
                    strain[5, column] = gradient[2]
                    strain[5, column + 2] = gradient[0]
                stiffness += strain.T @ elastic @ strain / 8.0
    return stiffness


def upper_shift(values):
    return jnp.concatenate([values[..., 1:], jnp.zeros_like(values[..., :1])], axis=-1)


def lower_shift(values):
    return jnp.concatenate([jnp.zeros_like(values[..., :1]), values[..., :-1]], axis=-1)


def corner_sum(corner_forces, rows_y, cols_z):
    total = None
    for corner, (a, b, c) in enumerate(CORNERS):
        term = corner_forces[
            3 * corner : 3 * corner + 3, 1 - a : 1 - a + rows_y, 1 - b : 1 - b + cols_z, :
        ]
        if c:
            term = lower_shift(term)
        total = term if total is None else total + term
    return total


def node_forces(node_halo, mod_halo, stiffness):
    rows_y = node_halo.shape[1] - 2
    cols_z = node_halo.shape[2] - 2
    pieces = []
    for a, b, c in CORNERS:
        piece = node_halo[:, a : a + rows_y + 1, b : b + cols_z + 1, :]
        pieces.append(upper_shift(piece) if c else piece)
    corner_values = jnp.concatenate(pieces, axis=0)
    moduli = mod_halo[: rows_y + 1, : cols_z + 1, :]
    corner_forces = moduli[None] * jnp.einsum(
        "pq,qyzx->pyzx", stiffness, corner_values, precision=HIGHEST
    )
    return corner_sum(corner_forces, rows_y, cols_z)


def node_diag(mod_halo, stiff_diag):
    rows_y = mod_halo.shape[0] - 2
    cols_z = mod_halo.shape[1] - 2
    moduli = mod_halo[: rows_y + 1, : cols_z + 1, :]
    corner_forces = moduli[None] * stiff_diag[:, None, None, None]
    return corner_sum(corner_forces, rows_y, cols_z)


def owned_corners(upper_nodes):
    rows_y = upper_nodes.shape[1] - 1
    cols_z = upper_nodes.shape[2] - 1
    pieces = []
    for a, b, c in CORNERS:
        piece = upper_nodes[:, a : a + rows_y, b : b + cols_z, :]
        pieces.append(upper_shift(piece) if c else piece)
    return jnp.concatenate(pieces, axis=0)


def dft_table(length):
    counter = jnp.arange(length, dtype=jnp.int32)
    phases = counter[:, None] * counter[None, :] % length
    angles = 2.0 * np.pi / length * phases.astype(jnp.float32)
    return jnp.concatenate([jnp.cos(angles), jnp.sin(angles)], axis=0)


def residual_inner(residual, precond):
    return lax.psum(jnp.sum(residual * precond), ("gy", "gz"))


def local(force, density, solid_blocks, fixed_nodes, filter_gain):
    stiffness = jnp.asarray(element_matrix(), jnp.float32)
    stiff_diag = jnp.diagonal(stiffness)
    rows_y = density.shape[0]
    cols_z = density.shape[1]
    solid = jnp.repeat(
        jnp.repeat(jnp.repeat(solid_blocks, 8, axis=0), 8, axis=1), 8, axis=2
    ).astype(jnp.float32)
    modulus = solid * (MIN_MODULUS + (1.0 - MIN_MODULUS) * density**3)
    free = (1 - fixed_nodes).astype(jnp.float32)[None]
    lower_y = passed_along(modulus[rows_y - 1 :], "gy", 1)
    mod_y = jnp.concatenate([lower_y, modulus], axis=0)
    lower_z = passed_along(mod_y[:, cols_z - 1 :], "gz", 1)
    mod_yz = jnp.concatenate([lower_z, mod_y], axis=1)
    mod_halo = jnp.pad(mod_yz, ((0, 1), (0, 1), (0, 0)))
    diag = node_diag(mod_halo, stiff_diag)
    inverse = 1.0 / jnp.maximum(diag, DIAG_FLOOR)
    displacement = jnp.zeros_like(force)
    residual = free * force
    precond = inverse * residual
    direction = precond
    rz_now = residual_inner(residual, precond)
    for step in range(ITERS):
        masked = free * direction
        node_halo = with_halo(masked, (("gy", 1), ("gz", 2)), 1)
        result = node_forces(node_halo, mod_halo, stiffness)
        image = free * result + (1.0 - free) * direction
        alpha = rz_now / lax.psum(jnp.sum(direction * image), ("gy", "gz"))
        displacement = displacement + alpha * direction
        residual = residual - alpha * image
        if step + 1 < ITERS:
            precond = inverse * residual
            rz_next = residual_inner(residual, precond)
            direction = precond + rz_next / rz_now * direction
            rz_now = rz_next
    top_y = passed_along(displacement[:, :1], "gy", -1)
    disp_y = jnp.concatenate([displacement, top_y], axis=1)
    top_z = passed_along(disp_y[:, :, :1], "gz", -1)
    disp_yz = jnp.concatenate([disp_y, top_z], axis=2)
    corner_values = owned_corners(disp_yz)
    applied = jnp.einsum("pq,qyzx->pyzx", stiffness, corner_values, precision=HIGHEST)
    energy = jnp.sum(corner_values * applied, axis=0)
    sensitivity = -3.0 * (1.0 - MIN_MODULUS) * density**2 * solid * energy
    weighted = density * sensitivity
    doubled_gain = jnp.concatenate([filter_gain, filter_gain], axis=0)
    line_weighted = lax.all_to_all(weighted, "gz", split_axis=0, concat_axis=1, tiled=True)
    line_density = lax.all_to_all(density, "gz", split_axis=0, concat_axis=1, tiled=True)
    length = line_weighted.shape[1]
    table = dft_table(length)
    spectrum = jnp.einsum("kn,ynx->ykx", table, line_weighted, precision=HIGHEST)
    spectrum = spectrum * doubled_gain[None, :, None]
    back = jnp.einsum("kn,ykx->ynx", table, spectrum, precision=HIGHEST) / length
    filtered = back / line_density
    return (displacement, filtered)


def solution(mesh):
    in_specs = (
        P(None, "gy", "gz", None),
        P("gy", "gz", None),
        P("gy", "gz", None),
        P("gy", "gz", None),
        P(),
    )
    out_specs = (P(None, "gy", "gz", None), P(("gy", "gz"), None, None))
    return jax.shard_map(local, mesh=mesh, in_specs=in_specs, out_specs=out_specs, check_vma=False)
```

profile of v0, /device:TPU:6, one launch (start us, length us, event | category | flops | bytes accessed | tf_op | source)
XLA Modules:
  0.0 812.1 jit_solution(8485709319411564170)
XLA Ops:
  5.1 4.3 collective-permute-start.1
  11.0 7.1 collective-permute-done.1
  21.8 3.5 collective-permute-start.2
  26.2 3.6 collective-permute-start.5
  29.8 2.2 collective-permute-start.4
  32.4 5.8 collective-permute-done.4
  44.7 39.2 %concatenate.180 = f32[24,33,9,128]{3,0,2,1:T(8,128)} concatenate(f32[3,33,9,128]{3,0,2,1:T(4,128)} %get-tuple-element.91, f32[3,33,9,128]{3,0,2,1:T(4,128)} %concatenate.175, f32[3,33,9,128]{3,0,2,1:T(4,128)S(1)} %get-tuple-element.60, f32[3,33,9,128]{3,0,2,1:T(4,128)} %concatenate.177, f32[3,33,9,128]{3,0,2,1:T(4,128)} %get-tuple-element.92, f32[3,33,9,128]{3,0,2,1:T(4,128)} %concatenate.178, ...), dimensions={0} | concatenate | bytes 7299072 | tf_op jit(solution)/shard_map/concatenate | solution.py:104
  83.9 5.4 multiply_bitcast_fusion.2
  89.8 2.2 multiply_reduce_fusion.4
  92.1 99.9 %all-reduce.32 = (f32[]{:T(128)}, f32[]{:T(128)}) all-reduce(f32[]{:T(128)} %get-tuple-element.9, f32[]{:T(128)} %get-tuple-element.8), channel_id=1, replica_groups=mesh['gy'=16,'gz'=32] {'gy','gz'}, use_global_device_ids=true, to_apply=%region_1.2 | all-reduce | flops 2 | bytes 16 | tf_op jit(solution)/shard_map/psum | solution.py:138
  195.2 96.8 %psum.44 = f32[]{:T(128)} all-reduce(f32[]{:T(128)} %get-tuple-element.18), channel_id=1, replica_groups=mesh['gy'=16,'gz'=32] {'gy','gz'}, use_global_device_ids=true, to_apply=%region_5.6 | all-reduce | flops 1 | bytes 8 | tf_op jit(solution)/shard_map/psum | solution.py:138
  295.9 3.0 collective-permute-start.6
  299.8 3.8 collective-permute-start.9
  303.7 2.0 collective-permute-start.8
  306.1 6.5 collective-permute-done.8
  320.1 39.1 %concatenate.192 = f32[24,33,9,128]{3,0,2,1:T(8,128)} concatenate(f32[3,33,9,128]{3,0,2,1:T(4,128)} %get-tuple-element.56, f32[3,33,9,128]{3,0,2,1:T(4,128)} %concatenate.187, f32[3,33,9,128]{3,0,2,1:T(4,128)} %get-tuple-element.52, f32[3,33,9,128]{3,0,2,1:T(4,128)} %concatenate.189, f32[3,33,9,128]{3,0,2,1:T(4,128)S(1)} %get-tuple-element.55, f32[3,33,9,128]{3,0,2,1:T(4,128)} %concatenate.190, ...), dimensions={0} | concatenate | bytes 7299072 | tf_op jit(solution)/shard_map/concatenate | solution.py:104
  359.2 5.4 multiply_bitcast_fusion.1
  367.2 97.7 %psum.45 = f32[]{:T(128)} all-reduce(f32[]{:T(128)} %get-tuple-element.14), channel_id=1, replica_groups=mesh['gy'=16,'gz'=32] {'gy','gz'}, use_global_device_ids=true, to_apply=%region_7.8 | all-reduce | flops 1 | bytes 8 | tf_op jit(solution)/shard_map/psum | solution.py:168
  467.3 95.0 %psum.46 = f32[]{:T(128)} all-reduce(f32[]{:T(128)} %multiply_reduce_fusion.1), channel_id=1, replica_groups=mesh['gy'=16,'gz'=32] {'gy','gz'}, use_global_device_ids=true, to_apply=%region_9.10 | all-reduce | flops 1 | bytes 8 | tf_op jit(solution)/shard_map/psum | solution.py:138
  566.4 3.0 collective-permute-start.10
  570.3 4.4 collective-permute-start.13
  577.1 6.5 collective-permute-done.12
  591.5 39.3 %concatenate.204 = f32[24,33,9,128]{3,0,2,1:T(8,128)} concatenate(f32[3,33,9,128]{3,0,2,1:T(4,128)} %get-tuple-element.48, f32[3,33,9,128]{3,0,2,1:T(4,128)} %concatenate.199, f32[3,33,9,128]{3,0,2,1:T(4,128)} %get-tuple-element.44, f32[3,33,9,128]{3,0,2,1:T(4,128)} %concatenate.201, f32[3,33,9,128]{3,0,2,1:T(4,128)} %get-tuple-element.47, f32[3,33,9,128]{3,0,2,1:T(4,128)} %concatenate.202, ...), dimensions={0} | concatenate | bytes 7299072 | tf_op jit(solution)/shard_map/concatenate | solution.py:104
  630.7 5.4 multiply_bitcast_fusion
  638.5 6.5 all-to-all-start.1
  644.9 98.0 %psum.47 = f32[]{:T(128)} all-reduce(f32[]{:T(128)} %fusion.26), channel_id=1, replica_groups=mesh['gy'=16,'gz'=32] {'gy','gz'}, use_global_device_ids=true, to_apply=%region_11.12 | all-reduce | flops 1 | bytes 8 | tf_op jit(solution)/shard_map/psum | solution.py:168
  747.7 3.3 collective-permute-start.15
  751.4 2.5 collective-permute-done.15
  756.1 28.9 %concatenate.215 = f32[24,32,8,128]{3,0,2,1:T(8,128)} concatenate(f32[3,32,8,128]{3,0,2,1:T(4,128)S(1)} %multiply_add_fusion, f32[3,32,8,128]{3,0,2,1:T(4,128)S(1)} %concatenate.209, f32[3,32,8,128]{3,0,2,1:T(4,128)} %get-tuple-element.68, f32[3,32,8,128]{3,0,2,1:T(4,128)S(1)} %concatenate.212, f32[3,32,8,128]{3,0,2,1:T(4,128)S(1)} %get-tuple-element.82, ...), dimensions={0} | concatenate | bytes 6291456 | tf_op jit(solution)/shard_map/concatenate | solution.py:127
  785.0 5.8 multiply_reduce_fusion
  792.4 8.1 all-to-all-start
  802.5 7.5 all-to-all-done
  (105 shorter events, 62.2 us)
Async XLA Ops:
  2.4 2.7 collective-permute-start
  5.1 12.9 %collective-permute-start.1 = (f32[33,1,128]{2,1,0:T(1,128)S(1)}, f32[33,1,128]{2,1,0:T(1,128)S(1)}, u32[]{:S(2)}, u32[]{:S(2)}) collective-permute-start(f32[33,1,128]{2,1,0:T(1,128)S(1)} %pad_maximum_fusion.17), channel_id=1, source_target_pairs={{0,1},{1,2},{2,3},{3,4},{4,5},{5,6},{6,7},{7,8},{8,9},{9,10},{10,1... | collective-permute-start | bytes 50696 | tf_op jit(solution)/shard_map/ppermute | solution.py:19
  18.1 1.0 copy-start.1
  19.1 13.0 %copy-start.2 = (s32[32,8,128]{2,1,0:T(8,128)S(1)}, s32[32,8,128]{2,1,0:T(8,128)}, u32[]{:S(2)}) copy-start(s32[32,8,128]{2,1,0:T(8,128)} %param.9) | copy-start | bytes 393220
  20.5 4.8 collective-permute-start.3
  21.8 4.4 collective-permute-start.2
  26.2 6.2 collective-permute-start.5
  29.8 8.3 %collective-permute-start.4 = (f32[3,34,1,128]{3,0,2,1:T(4,128)S(1)}, f32[3,34,1,128]{3,0,2,1:T(4,128)S(1)}, u32[]{:S(2)}, u32[]{:S(2)}) collective-permute-start(f32[3,34,1,128]{3,0,2,1:T(4,128)S(1)} %get-tuple-element.80), channel_id=1, source_target_pairs={{0,1},{1,2},{2,3},{3,4},{4,5},{5,6},{6,7},{7,8},{8,9},{9,10},{10,1... | collective-permute-start | bytes 156680 | tf_op jit(solution)/shard_map/ppermute | solution.py:29
  44.7 39.2 %copy-start.3 = (f32[24,24,1,1]{1,0,3,2:T(8,128)S(1)}, f32[24,24,1,1]{1,0,3,2:T(8,128)}, u32[]{:S(2)}) copy-start(f32[24,24,1,1]{1,0,3,2:T(8,128)} %constant.127) | copy-start | bytes 6916
  294.6 4.3 collective-permute-start.7
  295.9 3.9 collective-permute-start.6
  299.8 6.3 collective-permute-start.9
  303.7 8.9 %collective-permute-start.8 = (f32[3,34,1,128]{3,0,2,1:T(4,128)S(1)}, f32[3,34,1,128]{3,0,2,1:T(4,128)S(1)}, u32[]{:S(2)}, u32[]{:S(2)}) collective-permute-start(f32[3,34,1,128]{3,0,2,1:T(4,128)S(1)} %get-tuple-element.76), channel_id=1, source_target_pairs={{0,1},{1,2},{2,3},{3,4},{4,5},{5,6},{6,7},{7,8},{8,9},{9,10},{10,1... | collective-permute-start | bytes 156680 | tf_op jit(solution)/shard_map/ppermute | solution.py:29
  367.2 195.1 %copy-start = (f32[3,32,8,128]{3,0,2,1:T(4,128)}, f32[3,32,8,128]{3,0,2,1:T(4,128)S(1)}, u32[]{:S(2)}) copy-start(f32[3,32,8,128]{3,0,2,1:T(4,128)S(1)} %get-tuple-element.15) | copy-start | bytes 1179652
  565.1 4.3 collective-permute-start.11
  566.4 3.9 collective-permute-start.10
  570.3 6.8 collective-permute-start.13
  574.7 8.9 %collective-permute-start.12 = (f32[3,34,1,128]{3,0,2,1:T(4,128)S(1)}, f32[3,34,1,128]{3,0,2,1:T(4,128)S(1)}, u32[]{:S(2)}, u32[]{:S(2)}) collective-permute-start(f32[3,34,1,128]{3,0,2,1:T(4,128)S(1)} %get-tuple-element.72), channel_id=1, source_target_pairs={{0,1},{1,2},{2,3},{3,4},{4,5},{5,6},{6,7},{7,8},{8,9},{9,10},{10,1... | collective-permute-start | bytes 156680 | tf_op jit(solution)/shard_map/ppermute | solution.py:29
  638.5 153.9 %all-to-all-start.1 = ((f32[32,8,128]{2,1,0:T(8,128)}), f32[32,8,128]{2,1,0:T(8,128)S(1)}, u32[]{:S(2)}, u32[]{:S(2)}) async-start(f32[32,8,128]{2,1,0:T(8,128)} %param.7), calls=%async_computation.1 | async-start | bytes 262144 | tf_op jit(solution)/shard_map/all_to_all | solution.py:187
  744.6 3.1 collective-permute-start.14
  747.7 6.2 collective-permute-start.15
  785.0 15.5 %copy-start.4 = (f32[256]{0:T(256)S(1)}, f32[256]{0:T(256)}, u32[]{:S(2)}) copy-start(f32[256]{0:T(256)} %param.10) | copy-start | bytes 3076
  792.4 17.5 %all-to-all-start = ((f32[32,8,128]{2,1,0:T(8,128)}), f32[32,8,128]{2,1,0:T(8,128)S(1)}, u32[]{:S(2)}, u32[]{:S(2)}) async-start(f32[32,8,128]{2,1,0:T(8,128)} %fusion.39), calls=%async_computation | async-start | bytes 262144 | tf_op jit(solution)/shard_map/all_to_all | solution.py:186
where the time goes:
time: 828 us; the launch traced here: 812 us
  blocking collectives  487 us (59%)
  local copies, waits for them, and re-layouts  176 us (21%)
  starting transfers between devices  56.6 us (7%)
  waiting for transfers between devices  40.7 us (5%)
  matrix products  23.2 us (3%)
  other arithmetic  20.2 us (2%)
    psum x3, blocking collectives, residual_inner(): return lax.psum(jnp.sum(residual * precond), ('gy', 'gz'))  292 us
    psum x2, blocking collectives, local(): alpha = rz_now / lax.psum(jnp.sum(direction * image), ('gy', 'gz'))  196 us
    concatenate x3, local copies, waits for them, and re-layouts, node_forces(): corner_values = jnp.concatenate(pieces, axis=0)  118 us
    concatenate x1, local copies, waits for them, and re-layouts, owned_corners(): return jnp.concatenate(pieces, axis=0)  28.9 us
    ppermute x6, waiting for transfers between devices, with_halo(): before = lax.ppermute(last, axis, up)  21.2 us
  transfers between devices with their start and end apart: 18, of which 13 were waited for; matrix products, arithmetic and copies ran while one was open for 5% of the time, Pallas kernels for 0%

commit v1 on v0

v1 whole, which is shorter than its diff:
```python
import functools

import jax
import jax.numpy as jnp
import numpy as np
from jax import lax
from jax.experimental import pallas as pl
from jax.experimental.pallas import tpu as pltpu
from jax.sharding import PartitionSpec as P

MIN_MODULUS = 0.1
DIAG_FLOOR = 0.5
POISSON = 0.3
SHEAR = 1.0 / (2.0 * (1.0 + POISSON))
LAME = POISSON / ((1.0 + POISSON) * (1.0 - 2.0 * POISSON))
UNIT = SHEAR / 16.0
VOLUME = 0.5 * LAME / SHEAR
BEND = LAME / (3.0 * SHEAR)
TWIST = 1.0 / 3.0
WARP = (LAME + 4.0 * SHEAR) / 9.0 / SHEAR
KE_DIAG = (LAME + 4.0 * SHEAR) / 9.0
SHIFT = 1.0
PLANE = 16
FAR = 656
F32 = jnp.float32
HIGHEST = lax.Precision.HIGHEST
STEPS = [(-1, 0), (1, 0), (0, -1), (0, 1), (-1, -1), (-1, 1), (1, -1), (1, 1)]
LOWERS = (0, 2, 4)


def stress(y, z, x, m):
    m2, m3, m4 = 2.0 * m, TWIST * m, WARP * m
    gy, gz, gx = {}, {}, {}
    bulk = VOLUME * (y["100"] + z["010"] + x["001"])
    gy["100"] = m2 * (y["100"] + bulk)
    gz["010"] = m2 * (z["010"] + bulk)
    gx["001"] = m2 * (x["001"] + bulk)
    gy["010"] = gz["100"] = m * (y["010"] + z["100"])
    gz["001"] = gx["010"] = m * (z["001"] + x["010"])
    gy["001"] = gx["100"] = m * (y["001"] + x["100"])
    bend = BEND * (z["110"] + x["101"])
    gz["110"], gx["101"] = m * (z["110"] + bend), m * (x["101"] + bend)
    bend = BEND * (y["110"] + x["011"])
    gy["110"], gx["011"] = m * (y["110"] + bend), m * (x["011"] + bend)
    bend = BEND * (y["101"] + z["011"])
    gy["101"], gz["011"] = m * (y["101"] + bend), m * (z["011"] + bend)
    twist = y["011"] + z["101"] + x["110"]
    gy["011"] = m3 * (y["011"] + twist)
    gz["101"] = m3 * (z["101"] + twist)
    gx["110"] = m3 * (x["110"] + twist)
    gy["111"], gz["111"], gx["111"] = m4 * y["111"], m4 * z["111"], m4 * x["111"]
    return gy, gz, gx


def energy_of(coefs):
    total = None
    for c, g in zip(coefs, stress(*coefs, 1.0)):
        for key in g:
            term = c[key] * g[key]
            total = term if total is None else total + term
    return total


def pair_y(low, high):
    coefs = []
    for a, b in zip(low, high):
        c = {}
        for key in a:
            if key != "00":
                c["0" + key] = a[key] + b[key]
            c["1" + key] = b[key] - a[key]
        coefs.append(c)
    return coefs


def spread_y(g):
    low, high = {}, {}
    for key in ("00", "01", "10", "11"):
        d = g["1" + key]
        if key == "00":
            low[key], high[key] = -d, d
        else:
            s = g["0" + key]
            low[key], high[key] = s - d, s + d
    return low, high


def kernel(
    ny, nz, lines,
    force_h, dens_h, solid_h, fixed_h, gain_h, cos_h, sin_h,
    disp_h, filt_h,
    force, dens, solid, fixed, gain, cosine, sine,
    mod, mod_low, mod_stage, mod_face, mod_edge,
    inv, r0, w0, w1, v0, v1, v2, vx, low_z, low_zx,
    a_low, b_low, a_up, b_up, p_low, p_up, q_low, q_up,
    stage_z, stage_c, land_y, land_z, land_c,
    tmp, sums, acc, slots_y, slots_z,
    circ, weighted, line_w, line_d, disp, filt,
    load_sem, store_sem, mod_send, mod_recv, halo_send, halo_recv, sum_send, sum_recv, line_send, line_recv,
):
    iy, iz = lax.axis_index("gy"), lax.axis_index("gz")
    lane = lax.broadcasted_iota(jnp.int32, (8, 128), 1)
    first_lane, last_lane = lane == 0, lane == 127
    zeros = jnp.zeros((8, 128), F32)

    def at_upper(u):
        return jnp.where(last_lane, 0.0, pltpu.roll(u, 127, 1))

    def from_lower(u):
        return jnp.where(first_lane, 0.0, pltpu.roll(u, 1, 1))

    def modulus(e):
        return mod[pl.ds(8 * e if isinstance(e, int) else pl.multiple_of(8 * e, 8), 8), :]

    loads = [
        pltpu.make_async_copy(src, dst, load_sem.at[i])
        for i, (src, dst) in enumerate(
            [(dens_h, dens), (solid_h, solid), (fixed_h, fixed), (force_h, force), (gain_h, gain), (cos_h, cosine), (sin_h, sine)]
        )
    ]
    for load in loads:
        load.start()

    barrier = pltpu.get_barrier_semaphore()

    def greet_z(i, carry):
        pl.semaphore_signal(barrier, 1, device_id={"gz": lax.rem(iz + i, nz)})
        return carry

    def greet_y(i, carry):
        pl.semaphore_signal(barrier, 1, device_id={"gy": lax.rem(iy + i, ny)})
        return carry

    lax.fori_loop(1, nz, greet_z, 0)
    lax.fori_loop(1, ny, greet_y, 0)

    def there(step):
        sy, sz = step
        ok = None
        for index, s, n in ((iy, sy, ny), (iz, sz, nz)):
            if s:
                here = index >= 1 if s < 0 else index < n - 1
                ok = here if ok is None else jnp.logical_and(ok, here)
        return ok

    def device(step):
        return {"gy": iy + step[0], "gz": iz + step[1]}

    for sy, sz in STEPS[4:]:
        pl.semaphore_signal(barrier, 1, device_id={"gy": lax.rem(iy + sy + ny, ny), "gz": lax.rem(iz + sz + nz, nz)})

    loads[0].wait()
    loads[1].wait()
    flags = solid[:, 0, :].astype(F32)
    spread = (
        lax.broadcasted_iota(jnp.int32, (16, 128), 1) // 8 == lax.broadcasted_iota(jnp.int32, (16, 128), 0)
    ).astype(F32)
    solid_rows = jnp.dot(flags, spread, precision=HIGHEST, preferred_element_type=F32)
    for block in range(4):
        row = solid_rows[block : block + 1]
        for y in range(8 * block, 8 * block + 8):
            d = dens[y]
            mod[pl.ds(8 * (y + 1), 8), :] = row * (UNIT * MIN_MODULUS + (UNIT * (1.0 - MIN_MODULUS)) * (d * d * d))
    for j in range(4):
        mod_stage[pl.ds(8 * j, 8), :] = mod[pl.ds(8 * (8 * j + 1) + 7, 8, 8), :]

    pl.semaphore_wait(barrier, nz - 1 + ny - 1 + 4)

    mod_copies = []
    for i, (step, src, dst) in enumerate(
        [((1, 0), mod.at[pl.ds(256, 8)], mod.at[pl.ds(0, 8)]), ((0, 1), mod_stage, mod_face), ((1, 1), mod_stage.at[pl.ds(24, 8)], mod_edge)]
    ):
        down = (-step[0], -step[1])
        mod_copies.append((step, down, pltpu.make_async_remote_copy(
            src, dst, mod_send.at[i], mod_recv.at[i], device_id=device(step))))

    for step, down, copy in mod_copies:
        @pl.when(there(step))
        def _(copy=copy):
            copy.start()

    for (step, down, copy), fill in zip(mod_copies, (mod.at[pl.ds(0, 8)], mod_face, mod_edge)):
        @pl.when(jnp.logical_not(there(down)))
        def _(fill=fill):
            fill[...] = jnp.zeros(fill.shape, F32)

    def send_density(i, carry):
        to = lax.rem(iz + i, nz)
        pltpu.make_async_remote_copy(
            dens.at[pl.ds(to * lines, lines)], line_d.at[:, pl.ds(pl.multiple_of(iz * 8, 8), 8), :],
            line_send.at[0], line_recv.at[0], device_id={"gz": to},
        ).start()
        return carry

    lax.fori_loop(1, nz, send_density, 0)
    for i in range(lines):
        line_d[i, pl.ds(pl.multiple_of(iz * 8, 8), 8), :] = dens[iz * lines + i]

    for load in loads[4:]:
        load.wait()
    length = cosine.shape[0]
    gains = gain[...] * (1.0 / length)
    circ[...] = jnp.dot(cosine[...] * gains, cosine[...], precision=HIGHEST, preferred_element_type=F32) + jnp.dot(
        sine[...] * gains, sine[...], precision=HIGHEST, preferred_element_type=F32)

    loads[2].wait()
    loads[3].wait()

    def halo_copies(k, src, which):
        copies = []
        for i in which:
            sy, sz = STEPS[i]
            if sz == 0:
                s, d = src.at[:, pl.ds(PLANE * (1 if sy < 0 else 32), 8), :], land_y.at[k, i]
            elif sy == 0:
                s, d = stage_z.at[k, i - 2], land_z.at[k, i - 2]
            else:
                s, d = stage_c.at[k, i - 4], land_c.at[k, i - 4]
            copies.append((i, pltpu.make_async_remote_copy(
                s, d, halo_send.at[k, i], halo_recv.at[k, i], device_id=device(STEPS[i]))))
        return copies

    def send_halo(k, src, which):
        for c in range(3):
            for side, z in ((0, 0), (1, 7)):
                if side + 2 in which:
                    for j in range(4):
                        stage_z[k, side, c, pl.ds(8 * j, 8), :] = src[c, pl.ds(PLANE * (8 * j + 1) + z, 8, PLANE), :]
            for i in which:
                if i >= 4:
                    row = PLANE * (1 if STEPS[i][0] < 0 else 32) + (0 if STEPS[i][1] < 0 else 7)
                    stage_c[k, i - 4, pl.ds(c, 1), :] = src[c, pl.ds(row, 1), :]
        for i, copy in halo_copies(k, src, which):
            @pl.when(there(STEPS[i]))
            def _(copy=copy):
                copy.start()

    def land_of(k, i):
        return land_y.at[k, i] if i < 2 else land_z.at[k, i - 2] if i < 4 else land_c.at[k, i - 4]

    def clear_halo(k, which):
        for i in which:
            @pl.when(jnp.logical_not(there((-STEPS[i][0], -STEPS[i][1]))))
            def _(i=i):
                ref = land_of(k, i)
                ref[...] = jnp.zeros(ref.shape, F32)

    def wait_halo(k, src, which):
        for i, copy in halo_copies(k, src, which):
            @pl.when(there((-STEPS[i][0], -STEPS[i][1])))
            def _(copy=copy):
                copy.wait_recv()

    def wait_sent(k, src, which):
        for i, copy in halo_copies(k, src, which):
            @pl.when(there(STEPS[i]))
            def _(copy=copy):
                copy.wait_send()

    def put(ref, rows, u):
        ref[rows] = u
        vx[rows] = at_upper(u)

    def place_halo(k, ref, which):
        for c in range(3):
            put(ref, (c, pl.ds(PLANE * 33, 8), slice(None)), land_y[k, 0, c])
            if 1 in which:
                put(ref, (c, pl.ds(0, 8), slice(None)), land_y[k, 1, c])
            for j in range(4):
                rows = (c, pl.ds(PLANE * (8 * j + 1) + 8, 8, PLANE), slice(None))
                put(ref, rows, land_z[k, 0, c, pl.ds(8 * j, 8), :])
                if 3 in which:
                    u = land_z[k, 1, c, pl.ds(8 * j, 8), :]
                    low_z[c, pl.ds(8 * j + 1, 8), :] = u
                    low_zx[c, pl.ds(8 * j + 1, 8), :] = at_upper(u)
        for i in which:
            if i < 4:
                continue
            u = land_c[k, i - 4]
            ux = at_upper(u)
            y_row = 33 if STEPS[i][0] < 0 else 0
            for c in range(3):
                if STEPS[i][1] < 0:
                    ref[c, pl.ds(PLANE * y_row + 8, 1), :] = u[c : c + 1]
                    vx[c, pl.ds(PLANE * y_row + 8, 1), :] = ux[c : c + 1]
                else:
                    low_z[c, pl.ds(y_row, 1), :] = u[c : c + 1]
                    low_zx[c, pl.ds(y_row, 1), :] = ux[c : c + 1]

    def pair_zx(u0, x0, u1, x1):
        s0, d0, s1, d1 = u0 + x0, x0 - u0, u1 + x1, x1 - u1
        return {"00": s0 + s1, "01": d0 + d1, "10": s1 - s0, "11": d1 - d0}

    def plane(ref, row):
        row = pl.multiple_of(row, PLANE)
        return [
            pair_zx(ref[c, pl.ds(row, 8), :], vx[c, pl.ds(row, 8), :], ref[c, pl.ds(row + 1, 8), :], vx[c, pl.ds(row + 1, 8), :])
            for c in range(3)
        ]

    def low_layer(ref):
        for j in range(5):
            def rows(start):
                return [
                    pair_zx(
                        low_z[c, pl.ds(start, 8), :], low_zx[c, pl.ds(start, 8), :],
                        ref[c, pl.ds(PLANE * start, 8, PLANE), :], vx[c, pl.ds(PLANE * start, 8, PLANE), :])
                    for c in range(3)
                ]
            coefs = pair_y(rows(8 * j), rows(8 * j + 1))
            for c, g in enumerate(stress(*coefs, mod_low[pl.ds(8 * j, 8), :])):
                for part, start, pa, pb in zip(spread_y(g), (8 * j, 8 * j + 1), (p_low, p_up), (q_low, q_up)):
                    s, d = part["00"] + part["10"], part["01"] + part["11"]
                    pa[c, pl.ds(start, 8), :] = s - d
                    pb[c, pl.ds(start, 8), :] = s + d
        for c in range(3):
            for j in range(4):
                rows = pl.ds(8 * j + 1, 8)
                to = (c, pl.ds(PLANE * 8 * j, 8, PLANE), slice(None))
                a_up[to] = p_low[c, rows, :] + p_up[c, rows, :]
                b_up[to] = q_low[c, rows, :] + q_up[c, rows, :]

    def flat(planes):
        return tuple(p[key] for p in planes for key in ("00", "01", "10", "11"))

    def unflat(values):
        keys = ("00", "01", "10", "11")
        return [dict(zip(keys, values[4 * c : 4 * c + 4])) for c in range(3)]

    def forces(ref):
        low, high = plane(ref, 0), plane(ref, PLANE)
        upper = [spread_y(g)[1] for g in stress(*pair_y(low, high), modulus(0))]

        def one(e, low, upper):
            high = plane(ref, PLANE * (e + 1))
            new = []
            for c, g in enumerate(stress(*pair_y(low, high), modulus(e))):
                lo, hi = spread_y(g)
                t = {key: upper[c][key] + lo[key] for key in lo}
                new.append(hi)
                sa, sb, da, db = t["00"] - t["01"], t["00"] + t["01"], t["10"] - t["11"], t["10"] + t["11"]
                row = pl.multiple_of(PLANE * (e - 1), PLANE)
                a_low[c, e - 1] = sa - da
                b_low[c, e - 1] = sb - db
                a_up[c, pl.ds(row + 1, 8), :] = sa + da
                b_up[c, pl.ds(row + 1, 8), :] = sb + db
            return high, new

        def body(i, carry):
            low, upper = unflat(carry[:12]), unflat(carry[12:])
            for k in range(4):
                low, upper = one(4 * i + 1 + k, low, upper)
            return flat(low) + flat(upper)

        lax.fori_loop(0, 8, body, flat(high) + flat(upper))

    def finish(ref, image, after):
        def body(i, carry):
            for k in range(4):
                y = 4 * i + k
                held = fixed[y] != 0
                scale = inv[y]
                row = pl.multiple_of(PLANE * y, PLANE)
                for c in range(3):
                    f = (a_low[c, y] + a_up[c, pl.ds(row, 8), :]) + from_lower(b_low[c, y] + b_up[c, pl.ds(row, 8), :])
                    v = ref[c, pl.ds(row + PLANE, 8), :]
                    w = jnp.where(held, v, f)
                    image[c, y] = w
                    new = scale * w - SHIFT * v
                    after[c, pl.ds(row + PLANE, 8), :] = new
                    vx[c, pl.ds(row + PLANE, 8), :] = at_upper(new)
            return carry
        lax.fori_loop(0, 8, body, 0)

    def dots(pairs):
        def get(ref, c, y):
            if ref.shape[1] == FAR:
                return ref[c, pl.ds(pl.multiple_of(PLANE * y + PLANE, PLANE), 8), :]
            return ref[c, y]

        def body(i, carry):
            carry = list(carry)
            for k in range(2):
                for c in range(3):
                    held = {}
                    for p, (slot, a, b) in enumerate(pairs):
                        for ref in (a, b):
                            if id(ref) not in held:
                                held[id(ref)] = get(ref, c, 2 * i + k)
                        carry[p] = carry[p] + held[id(a)] * held[id(b)]
            return tuple(carry)

        total = lax.fori_loop(0, 16, body, (zeros,) * len(pairs))
        for (slot, a, b), t in zip(pairs, total):
            acc[pl.ds(slot, 1), :] = jnp.sum(t, axis=0, keepdims=True)

    for c in range(3):
        def body(i, carry, c=c):
            for k in range(4):
                y = 4 * i + k
                r0[c, y] = jnp.where(fixed[y] != 0, 0.0, force[c, y])
            return carry
        lax.fori_loop(0, 8, body, 0)
    every = tuple(range(8))
    clear_halo(0, every)
    clear_halo(1, every)
    clear_halo(2, LOWERS)
    acc[...] = jnp.zeros(acc.shape, F32)

    for step, down, copy in mod_copies:
        @pl.when(there(down))
        def _(copy=copy):
            copy.wait_recv()

    for j in range(4):
        mod_low[pl.ds(8 * j + 1, 8), :] = mod_face[pl.ds(8 * j, 8), :]
    mod_low[pl.ds(0, 1), :] = mod_edge[pl.ds(7, 1), :]
    for j in range(4):
        tmp[pl.ds(PLANE * 8 * j, 8, PLANE), :] = mod_low[pl.ds(8 * j, 8), :] + mod_low[pl.ds(8 * j + 1, 8), :]

    def sum_moduli(i, carry):
        for k in range(4):
            y = 4 * i + k
            t = modulus(y) + modulus(y + 1)
            sums[y] = t
            tmp[pl.ds(pl.multiple_of(PLANE * y, PLANE) + 1, 8), :] = t
        return carry
    lax.fori_loop(0, 8, sum_moduli, 0)

    def start(i, carry):
        for k in range(4):
            y = 4 * i + k
            t = sums[y] + tmp[pl.ds(pl.multiple_of(PLANE * y, PLANE), 8), :]
            t = t + from_lower(t)
            scale = 1.0 / jnp.maximum((KE_DIAG / UNIT) * t, DIAG_FLOOR)
            inv[y] = scale
            row = pl.multiple_of(PLANE * y + PLANE, PLANE)
            for c in range(3):
                v = scale * r0[c, y]
                v0[c, pl.ds(row, 8), :] = v
                vx[c, pl.ds(row, 8), :] = at_upper(v)
        return carry
    lax.fori_loop(0, 8, start, 0)

    send_halo(0, v0, every)
    dots([(0, r0, v0)])
    wait_halo(0, v0, every)
    place_halo(0, v0, every)
    low_layer(v0)
    forces(v0)
    finish(v0, w0, v1)
    send_halo(1, v1, every)
    dots([(1, r0, v1), (3, v0, w0), (4, v1, w0)])
    wait_halo(1, v1, every)
    place_halo(1, v1, every)
    low_layer(v1)
    forces(v1)
    finish(v1, w1, v2)
    send_halo(2, v2, LOWERS)
    dots([(2, r0, v2), (5, v2, w0), (6, v1, w1), (7, v2, w1)])
    wait_halo(2, v2, LOWERS)
    place_halo(2, v2, LOWERS)
    wait_sent(0, v0, every)

    def stored_energy(i, carry):
        low, total = unflat(carry[:12]), carry[12]
        for k in range(4):
            e = 4 * i + 1 + k
            high = plane(v2, PLANE * (e + 1))
            total = total + modulus(e) * energy_of(pair_y(low, high))
            low = high
        return flat(low) + (total,)
    total = lax.fori_loop(0, 8, stored_energy, flat(plane(v2, PLANE)) + (zeros,))[12]
    acc[pl.ds(8, 1), :] = jnp.sum(total, axis=0, keepdims=True)

    column = jnp.sum(acc[...], axis=1, keepdims=True)
    rows = lax.broadcasted_iota(jnp.int32, (16, 128), 0)
    lanes = lax.broadcasted_iota(jnp.int32, (16, 128), 1)
    part = jnp.sum(jnp.where(rows == lanes, column, 0.0), axis=0, keepdims=True)
    for k, (axis, me, n, slots) in enumerate((("gy", iy, ny, slots_y), ("gz", iz, nz, slots_z))):
        slots[me] = part

        def send_sum(i, carry, k=k, axis=axis, me=me, n=n, slots=slots):
            pltpu.make_async_remote_copy(
                slots.at[me], slots.at[me], sum_send.at[k], sum_recv.at[k], device_id={axis: lax.rem(me + i, n)},
            ).start()
            return carry
        lax.fori_loop(1, n, send_sum, 0)
        whole = slots.at[pl.ds(0, n - 1)]
        pltpu.make_async_copy(whole, whole, sum_recv.at[k]).wait()
        part = jnp.sum(slots[:, 0, :], axis=0, keepdims=True)

    lane1 = lax.broadcasted_iota(jnp.int32, (1, 128), 1)

    def entry(i):
        return jnp.sum(jnp.where(lane1 == i, part, 0.0), axis=1, keepdims=True)

    b0, b1, b2, g00, g10, g20, g11, g21, g22 = (entry(i) for i in range(9))
    l10, l20 = g10 / g00, g20 / g00
    d1 = g11 - l10 * g10
    e21 = g21 - l20 * g10
    l21 = e21 / d1
    d2 = g22 - l20 * g20 - l21 * e21
    y1 = b1 - l10 * b0
    y2 = b2 - l20 * b0 - l21 * y1
    c2 = y2 / d2
    c1 = y1 / d1 - l21 * c2
    c0 = b0 / g00 - l10 * c1 - l20 * c2
    c0, c1, c2 = (jnp.broadcast_to(c, (8, 128)) for c in (c0, c1, c2))

    def combine(yy, c, off):
        rows = (c, pl.ds(pl.multiple_of(PLANE * yy, PLANE) + off, 8), slice(None))
        u = c0 * v0[rows] + c1 * v1[rows] + c2 * v2[rows]
        v0[rows] = u
        vx[rows] = at_upper(u)
        return u

    def displace(i, carry):
        for k in range(4):
            for c in range(3):
                disp[c, 4 * i + k] = combine(4 * i + k + 1, c, 0)
                combine(4 * i + k + 1, c, 8)
        return carry
    lax.fori_loop(0, 8, displace, 0)
    for c in range(3):
        combine(33, c, 0)
        combine(33, c, 8)
    disp_copy = pltpu.make_async_copy(disp, disp_h, store_sem.at[0])
    disp_copy.start()

    solid_scale = (-3.0 * (1.0 - MIN_MODULUS) * UNIT) * solid_rows

    def sensitivities(block):
        def body(i, carry):
            low = unflat(carry)
            for k in range(4):
                y = 8 * block + 4 * i + k
                high = plane(v0, PLANE * (y + 2))
                d = dens[y]
                weighted[y] = (solid_scale[block : block + 1] * (d * d * d)) * energy_of(pair_y(low, high))
                low = high
            return flat(low)
        return body
    carry = flat(plane(v0, PLANE))
    for block in range(4):
        carry = lax.fori_loop(0, 2, sensitivities(block), carry)

    def send_weighted(i, carry):
        to = lax.rem(iz + i, nz)
        pltpu.make_async_remote_copy(
            weighted.at[pl.ds(to * lines, lines)], line_w.at[:, pl.ds(pl.multiple_of(iz * 8, 8), 8), :],
            line_send.at[1], line_recv.at[1], device_id={"gz": to},
        ).start()
        return carry
    lax.fori_loop(1, nz, send_weighted, 0)
    for i in range(lines):
        line_w[i, pl.ds(pl.multiple_of(iz * 8, 8), 8), :] = weighted[iz * lines + i]

    others = [ref.at[:, pl.ds(0, 8 * (nz - 1)), :] for ref in (line_d, line_w)]
    for k in range(2):
        pltpu.make_async_copy(others[k], others[k], line_recv.at[k]).wait()
    for i in range(lines):
        back = jnp.dot(circ[...], line_w[i], precision=HIGHEST, preferred_element_type=F32)
        filt[i] = back / line_d[i]
    filt_copy = pltpu.make_async_copy(filt, filt_h, store_sem.at[1])
    filt_copy.start()

    for k in range(2):
        pltpu.make_async_copy(others[k], others[k], line_send.at[k]).wait()
    for k, (n, slots) in enumerate(((ny, slots_y), (nz, slots_z))):
        whole = slots.at[pl.ds(0, n - 1)]
        pltpu.make_async_copy(whole, whole, sum_send.at[k]).wait()
    for step, down, copy in mod_copies:
        @pl.when(there(step))
        def _(copy=copy):
            copy.wait_send()
    wait_sent(1, v1, every)
    wait_sent(2, v2, LOWERS)
    disp_copy.wait()
    filt_copy.wait()


def solution(mesh):
    ny, nz = mesh.shape["gy"], mesh.shape["gz"]
    lines = 32 // nz
    length = 8 * nz
    phases = np.outer(np.arange(length), np.arange(length)) % length
    cosine = np.cos(2.0 * np.pi / length * phases).astype(np.float32)
    sine = np.sin(2.0 * np.pi / length * phases).astype(np.float32)

    def local(force, density, solid_blocks, fixed_nodes, filter_gain):
        vmem = lambda *shape: pltpu.VMEM(shape, F32)
        dma = lambda *shape: pltpu.SemaphoreType.DMA(shape)
        node = [vmem(3, FAR, 128)]
        return pl.pallas_call(
            functools.partial(kernel, ny, nz, lines),
            out_shape=(
                jax.ShapeDtypeStruct((3, 32, 8, 128), F32),
                jax.ShapeDtypeStruct((lines, length, 128), F32),
            ),
            in_specs=[pl.BlockSpec(memory_space=pl.ANY)] * 7,
            out_specs=(pl.BlockSpec(memory_space=pl.ANY),) * 2,
            scratch_shapes=[
                vmem(3, 32, 8, 128), vmem(32, 8, 128), pltpu.VMEM((4, 1, 16), jnp.int32), pltpu.VMEM((32, 8, 128), jnp.int32),
                vmem(1, length), vmem(length, length), vmem(length, length),
                vmem(264, 128), vmem(48, 128), vmem(32, 128), vmem(32, 128), vmem(8, 128),
                vmem(32, 8, 128), vmem(3, 32, 8, 128), vmem(3, 32, 8, 128), vmem(3, 32, 8, 128),
                *(node * 4), vmem(3, 48, 128), vmem(3, 48, 128),
                vmem(3, 32, 8, 128), vmem(3, 32, 8, 128), vmem(3, 512, 128), vmem(3, 512, 128),
                vmem(3, 48, 128), vmem(3, 48, 128), vmem(3, 48, 128), vmem(3, 48, 128),
                vmem(3, 2, 3, 32, 128), vmem(3, 4, 8, 128), vmem(3, 2, 3, 8, 128), vmem(3, 2, 3, 32, 128), vmem(3, 4, 8, 128),
                vmem(512, 128), vmem(32, 8, 128), vmem(16, 128), vmem(ny, 1, 128), vmem(nz, 1, 128),
                vmem(length, length), vmem(32, 8, 128), vmem(lines, length, 128), vmem(lines, length, 128),
                vmem(3, 32, 8, 128), vmem(lines, length, 128),
                dma(7), dma(2), dma(3), dma(3), dma(3, 8), dma(3, 8), dma(2), dma(2), dma(2), dma(2),
            ],
            compiler_params=pltpu.CompilerParams(collective_id=0, has_side_effects=True, vmem_limit_bytes=40 * 1024 * 1024),
            cost_estimate=pl.CostEstimate(flops=60_000_000, bytes_accessed=2_000_000, transcendentals=0),
        )(force, density, solid_blocks, fixed_nodes, filter_gain[None, :], jnp.asarray(cosine), jnp.asarray(sine))

    in_specs = (P(None, "gy", "gz", None), P("gy", "gz", None), P("gy", "gz", None), P("gy", "gz", None), P())
    out_specs = (P(None, "gy", "gz", None), P(("gy", "gz"), None, None))
    return jax.shard_map(local, mesh=mesh, in_specs=in_specs, out_specs=out_specs, check_vma=False)
```

time: 828 us -> 66 us (0.08); the launches traced: 812 us -> 65.7 us
  blocking collectives: 487 us -> 0 us
  local copies, waits for them, and re-layouts: 176 us -> 7.46 us
  Pallas kernels: 0 us -> 57.6 us
  starting transfers between devices: 56.6 us -> 0 us
  waiting for transfers between devices: 40.7 us -> 0 us
  matrix products: 23.2 us -> 0 us
  other arithmetic: 20.2 us -> 0 us
    psum x5 -> x0, blocking collectives: 487 us -> none  [the longest x3 292 us: residual_inner(): return lax.psum(jnp.sum(residual * precond), ('gy', 'gz'))]
    concatenate x19 -> x0, local copies, waits for them, and re-layouts: 158 us -> none  [the longest x3 118 us: node_forces(): corner_values = jnp.concatenate(pieces, axis=0)]
    pallas_call x0 -> x1, Pallas kernels: none -> 57.6 us  [local(): pl.pallas_call(functools.partial(kernel, ny, nz, lines), out_shape=(jax.S...]
    ppermute x16 -> x0, starting transfers between devices: 42.1 us -> none  [the longest x6 15.8 us: with_halo(): after = lax.ppermute(first, axis, down)]
    ppermute x16 -> x0, waiting for transfers between devices: 33.2 us -> none  [the longest x6 21.2 us: with_halo(): before = lax.ppermute(last, axis, up)]
    dot_general x6 -> x0, matrix products: 23.2 us -> none  [the longest x3 16.3 us: node_forces(): jnp.einsum('pq,qyzx->pyzx', stiffness, corner_values, precision=HIGHEST)]
    all_to_all x2 -> x0, starting transfers between devices: 14.6 us -> none  [the longest x1 8.11 us: local(): lax.all_to_all(weighted, 'gz', split_axis=0, concat_axis=1, tiled=True)]
    slice x22 -> x0, local copies, waits for them, and re-layouts: 14.5 us -> none  [the longest x5 5.93 us: node_forces(): piece = node_halo[:, a:a + rows_y + 1, b:b + cols_z + 1, :]]
  transfers between devices with their start and end apart: 18 -> 0, of which waited for: 13 -> 0; matrix products, arithmetic and copies ran while one was open for 5% -> 0% of each run, Pallas kernels for 0% -> 0%
where the time goes in v1:
time: 66 us; the launch traced here: 65.7 us
  Pallas kernels  57.6 us (87%)
  local copies, waits for them, and re-layouts  7.46 us (11%)
    pallas_call x1, Pallas kernels, local(): pl.pallas_call(functools.partial(kernel, ny, nz, lines), out_shape=(jax.S...  57.6 us
    unnamed x16, local copies, waits for them, and re-layouts  7.46 us

profile of v1, /device:TPU:6, one launch (start us, length us, event | category | flops | bytes accessed | tf_op | source)
XLA Modules:
  0.0 65.7 jit_solution(1346041656703837754)
XLA Ops:
  0.6 0.0 copy-start.6
  0.6 0.7 %copy-done.6 = f32[256]{0:T(256)S(1)} copy-done((f32[256]{0:T(256)S(1)}, f32[256]{0:T(256)}, u32[]{:S(2)}) %copy-start.6) | copy-done | bytes 1048
  1.3 0.0 copy-start
  1.3 1.0 %copy-done = f32[3,32,8,128]{3,2,1,0:T(8,128)S(1)} copy-done((f32[3,32,8,128]{3,2,1,0:T(8,128)S(1)}, f32[3,32,8,128]{3,2,1,0:T(8,128)}, u32[]{:S(2)}) %copy-start) | copy-done | bytes 393240
  2.3 0.0 copy-start.1
  2.3 0.9 %copy-done.1 = f32[256,256]{1,0:T(8,128)S(1)} copy-done((f32[256,256]{1,0:T(8,128)S(1)}, f32[256,256]{1,0:T(8,128)}, u32[]{:S(2)}) %copy-start.1) | copy-done | bytes 262168
  3.3 0.0 copy-start.2
  3.3 0.9 %copy-done.2 = f32[256,256]{1,0:T(8,128)S(1)} copy-done((f32[256,256]{1,0:T(8,128)S(1)}, f32[256,256]{1,0:T(8,128)}, u32[]{:S(2)}) %copy-start.2) | copy-done | bytes 262168
  4.2 0.0 copy-start.3
  4.2 0.9 %copy-done.3 = f32[32,8,128]{2,1,0:T(8,128)S(1)} copy-done((f32[32,8,128]{2,1,0:T(8,128)S(1)}, f32[32,8,128]{2,1,0:T(8,128)}, u32[]{:S(2)}) %copy-start.3) | copy-done | bytes 131096
  5.1 0.0 copy-start.4
  5.1 0.9 %copy-done.4 = s32[32,8,128]{2,1,0:T(8,128)S(1)} copy-done((s32[32,8,128]{2,1,0:T(8,128)S(1)}, s32[32,8,128]{2,1,0:T(8,128)}, u32[]{:S(2)}) %copy-start.4) | copy-done | bytes 131096
  6.0 0.0 copy-start.5
  6.0 0.7 %copy-done.5 = s32[4,1,16]{2,1,0:T(1,128)S(1)} copy-done((s32[4,1,16]{2,1,0:T(1,128)S(1)}, s32[4,1,16]{2,1,0:T(1,128)}, u32[]{:S(2)}) %copy-start.5) | copy-done | bytes 280
  6.7 57.6 %shard_map.86 = (f32[3,32,8,128]{3,2,1,0:T(8,128)S(1)}, f32[1,256,128]{2,1,0:T(8,128)S(1)}) custom-call(f32[3,32,8,128]{3,2,1,0:T(8,128)S(1)} %copy-done, f32[32,8,128]{2,1,0:T(8,128)S(1)} %copy-done.3, s32[4,1,16]{2,1,0:T(1,128)S(1)} %copy-done.5, s32[32,8,128]{2,1,0:T(8,128)S(1)} %copy-done.4, f32[1,256]{1,0:T(1,128)S(1)} %bitcast.1, ...), custom_call_target="tpu_custom_call" | custom-call | flops 60000000 | bytes 2000000 | tf_op jit(solution)/shard_map/pallas_call | solution.py:595
  64.3 0.7 %copy.11 = f32[3,32,8,128]{3,2,1,0:T(8,128)} copy(f32[3,32,8,128]{3,2,1,0:T(8,128)S(1)} %get-tuple-element.4) | data formatting | bytes 786432
  65.1 0.7 copy.12
Async XLA Ops:
  0.6 0.7 %copy-start.6 = (f32[256]{0:T(256)S(1)}, f32[256]{0:T(256)}, u32[]{:S(2)}) copy-start(f32[256]{0:T(256)} %param.11) | copy-start | bytes 3076
  1.3 1.0 %copy-start = (f32[3,32,8,128]{3,2,1,0:T(8,128)S(1)}, f32[3,32,8,128]{3,2,1,0:T(8,128)}, u32[]{:S(2)}) copy-start(f32[3,32,8,128]{3,2,1,0:T(8,128)} %force_h.1) | copy-start | bytes 1179652
  2.3 0.9 %copy-start.1 = (f32[256,256]{1,0:T(8,128)S(1)}, f32[256,256]{1,0:T(8,128)}, u32[]{:S(2)}) copy-start(f32[256,256]{1,0:T(8,128)} %constant.5.clone.sin_h) | copy-start | bytes 786436
  3.3 0.9 %copy-start.2 = (f32[256,256]{1,0:T(8,128)S(1)}, f32[256,256]{1,0:T(8,128)}, u32[]{:S(2)}) copy-start(f32[256,256]{1,0:T(8,128)} %constant.4.clone.cos_h) | copy-start | bytes 786436
  4.2 0.9 %copy-start.3 = (f32[32,8,128]{2,1,0:T(8,128)S(1)}, f32[32,8,128]{2,1,0:T(8,128)}, u32[]{:S(2)}) copy-start(f32[32,8,128]{2,1,0:T(8,128)} %dens_h.1) | copy-start | bytes 393220
  5.1 0.9 %copy-start.4 = (s32[32,8,128]{2,1,0:T(8,128)S(1)}, s32[32,8,128]{2,1,0:T(8,128)}, u32[]{:S(2)}) copy-start(s32[32,8,128]{2,1,0:T(8,128)} %fixed_h.1) | copy-start | bytes 393220
  6.0 0.7 %copy-start.5 = (s32[4,1,16]{2,1,0:T(1,128)S(1)}, s32[4,1,16]{2,1,0:T(1,128)}, u32[]{:S(2)}) copy-start(s32[4,1,16]{2,1,0:T(1,128)} %solid_h.1) | copy-start | bytes 772

commit v2 on v1

--- a/solution.py
+++ b/solution.py
@@ -52,9 +52,12 @@
     return gy, gz, gx
 
 
-def energy_of(coefs):
+FORMS = ((0, 0), (0, 1), (1, 1), (2, 0), (2, 1), (2, 2))
+
+
+def dot_forms(coefs, pulled):
     total = None
-    for c, g in zip(coefs, stress(*coefs, 1.0)):
+    for c, g in zip(coefs, pulled):
         for key in g:
             term = c[key] * g[key]
             total = term if total is None else total + term
@@ -90,13 +93,14 @@
     force_h, dens_h, solid_h, fixed_h, gain_h, cos_h, sin_h,
     disp_h, filt_h,
     force, dens, solid, fixed, gain, cosine, sine,
-    mod, mod_low, mod_stage, mod_face, mod_edge,
-    inv, r0, w0, w1, v0, v1, v2, vx, low_z, low_zx,
+    mod, mod_z, sum_low, sum_high, high_z,
+    inv, r0, w0, w1, v0, v1, v2, x0, x1, x2, low_z, low_zx,
     a_low, b_low, a_up, b_up, p_low, p_up, q_low, q_up,
+    first_y, first_z, first_c, seen_y, seen_z, seen_c,
     stage_z, stage_c, land_y, land_z, land_c,
-    tmp, sums, acc, slots_y, slots_z,
+    tmp, sums, acc, slots_y, slots_z, forms,
     circ, weighted, line_w, line_d, disp, filt,
-    load_sem, store_sem, mod_send, mod_recv, halo_send, halo_recv, sum_send, sum_recv, line_send, line_recv,
+    load_sem, store_sem, first_send, first_recv, halo_send, halo_recv, sum_send, sum_recv, line_send, line_recv,
 ):
     iy, iz = lax.axis_index("gy"), lax.axis_index("gz")
     lane = lax.broadcasted_iota(jnp.int32, (8, 128), 1)
@@ -123,6 +127,12 @@
 
     barrier = pltpu.get_barrier_semaphore()
 
+    def ring(sy, sz):
+        return {"gy": lax.rem(iy + sy + ny, ny), "gz": lax.rem(iz + sz + nz, nz)}
+
+    for sy, sz in STEPS:
+        pl.semaphore_signal(barrier, 1, device_id=ring(sy, sz))
+
     def greet_z(i, carry):
         pl.semaphore_signal(barrier, 1, device_id={"gz": lax.rem(iz + i, nz)})
         return carry
@@ -131,8 +141,8 @@
         pl.semaphore_signal(barrier, 1, device_id={"gy": lax.rem(iy + i, ny)})
         return carry
 
-    lax.fori_loop(1, nz, greet_z, 0)
-    lax.fori_loop(1, ny, greet_y, 0)
+    lax.fori_loop(2, nz - 1, greet_z, 0)
+    lax.fori_loop(2, ny - 1, greet_y, 0)
 
     def there(step):
         sy, sz = step
@@ -145,9 +155,6 @@
 
     def device(step):
         return {"gy": iy + step[0], "gz": iz + step[1]}
-
-    for sy, sz in STEPS[4:]:
-        pl.semaphore_signal(barrier, 1, device_id={"gy": lax.rem(iy + sy + ny, ny), "gz": lax.rem(iz + sz + nz, nz)})
 
     loads[0].wait()
     loads[1].wait()
@@ -161,40 +168,84 @@
         for y in range(8 * block, 8 * block + 8):
             d = dens[y]
             mod[pl.ds(8 * (y + 1), 8), :] = row * (UNIT * MIN_MODULUS + (UNIT * (1.0 - MIN_MODULUS)) * (d * d * d))
-    for j in range(4):
-        mod_stage[pl.ds(8 * j, 8), :] = mod[pl.ds(8 * (8 * j + 1) + 7, 8, 8), :]
-
-    pl.semaphore_wait(barrier, nz - 1 + ny - 1 + 4)
-
-    mod_copies = []
-    for i, (step, src, dst) in enumerate(
-        [((1, 0), mod.at[pl.ds(256, 8)], mod.at[pl.ds(0, 8)]), ((0, 1), mod_stage, mod_face), ((1, 1), mod_stage.at[pl.ds(24, 8)], mod_edge)]
-    ):
-        down = (-step[0], -step[1])
-        mod_copies.append((step, down, pltpu.make_async_remote_copy(
-            src, dst, mod_send.at[i], mod_recv.at[i], device_id=device(step))))
-
-    for step, down, copy in mod_copies:
-        @pl.when(there(step))
-        def _(copy=copy):
-            copy.start()
-
-    for (step, down, copy), fill in zip(mod_copies, (mod.at[pl.ds(0, 8)], mod_face, mod_edge)):
-        @pl.when(jnp.logical_not(there(down)))
-        def _(fill=fill):
-            fill[...] = jnp.zeros(fill.shape, F32)
-
-    def send_density(i, carry):
-        to = lax.rem(iz + i, nz)
+
+    loads[2].wait()
+    loads[3].wait()
+    for c in range(3):
+        def body(i, carry, c=c):
+            for k in range(4):
+                y = 4 * i + k
+                r0[pl.ds(pl.multiple_of(256 * c + 8 * y, 8), 8), :] = jnp.where(fixed[y] != 0, 0.0, force[c, y])
+            return carry
+        lax.fori_loop(0, 8, body, 0)
+
+    for side, y, moduli in ((0, 0, (0,)), (1, 31, (30, 31))):
+        for c in range(3):
+            first_y[side, c] = r0[pl.ds(256 * c + 8 * y, 8), :]
+        for k, e in enumerate(moduli):
+            first_y[side, 3 + k] = modulus(e + 1)
+    for side, z, moduli in ((0, 0, (0,)), (1, 7, (6, 7))):
+        for j in range(4):
+            rows = pl.ds(8 * j, 8)
+            for c in range(3):
+                first_z[side, c, rows, :] = r0[pl.ds(256 * c + 64 * j + z, 8, 8), :]
+            for k, e in enumerate(moduli):
+                first_z[side, 3 + k, rows, :] = mod[pl.ds(64 * j + 8 + e, 8, 8), :]
+    for i, (sy, sz) in enumerate(STEPS[4:]):
+        for c in range(3):
+            first_c[i, pl.ds(c, 1), :] = r0[pl.ds(256 * c + 8 * (0 if sy < 0 else 31) + (0 if sz < 0 else 7), 1), :]
+        spots = [(y, z) for y in ((0,) if sy < 0 else (30, 31)) for z in ((0,) if sz < 0 else (6, 7))]
+        for k, (y, z) in enumerate(spots):
+            first_c[i, pl.ds(3 + k, 1), :] = mod[pl.ds(8 * (y + 1) + z, 1), :]
+
+    pl.semaphore_wait(barrier, 8 + max(nz - 3, 0) + max(ny - 3, 0))
+
+    def part_of(arrays, i):
+        return arrays[0].at[i] if i < 2 else arrays[1].at[i - 2] if i < 4 else arrays[2].at[i - 4]
+
+    seen = (seen_y, seen_z, seen_c)
+    first_copies = [
         pltpu.make_async_remote_copy(
-            dens.at[pl.ds(to * lines, lines)], line_d.at[:, pl.ds(pl.multiple_of(iz * 8, 8), 8), :],
+            part_of((first_y, first_z, first_c), i), part_of(seen, i), first_send.at[i], first_recv.at[i],
+            device_id=device(step))
+        for i, step in enumerate(STEPS)
+    ]
+    ORDER = (7, 6, 5, 4, 2, 3, 0, 1)
+    for i in ORDER:
+        @pl.when(there(STEPS[i]))
+        def _(i=i):
+            first_copies[i].start()
+
+    def away(i):
+        return jnp.logical_not(there((-STEPS[i][0], -STEPS[i][1])))
+
+    for i in range(8):
+        @pl.when(away(i))
+        def _(i=i):
+            ref = part_of(seen, i)
+            ref[...] = jnp.zeros(ref.shape, F32)
+
+    rows_x = max(nz // 8, 1)
+    cols_z = nz // rows_x
+
+    def hops(i):
+        dx, dz = i // cols_z, i % cols_z
+        return -(min(dx, rows_x - dx) + min(dz, cols_z - dz))
+
+    def other_z(i):
+        x = lax.rem(iz // cols_z + i // cols_z, rows_x)
+        return x * cols_z + lax.rem(iz + i % cols_z, cols_z)
+
+    far_first = sorted(range(1, nz), key=hops)
+    mine = pl.ds(pl.multiple_of(iz * 8, 8), 8)
+    for i in far_first:
+        to = other_z(i)
+        pltpu.make_async_remote_copy(
+            dens.at[pl.ds(to * lines, lines)], line_d.at[:, mine, :],
             line_send.at[0], line_recv.at[0], device_id={"gz": to},
         ).start()
-        return carry
-
-    lax.fori_loop(1, nz, send_density, 0)
     for i in range(lines):
-        line_d[i, pl.ds(pl.multiple_of(iz * 8, 8), 8), :] = dens[iz * lines + i]
+        line_d[i, mine, :] = dens[iz * lines + i]
 
     for load in loads[4:]:
         load.wait()
@@ -202,9 +253,6 @@
     gains = gain[...] * (1.0 / length)
     circ[...] = jnp.dot(cosine[...] * gains, cosine[...], precision=HIGHEST, preferred_element_type=F32) + jnp.dot(
         sine[...] * gains, sine[...], precision=HIGHEST, preferred_element_type=F32)
-
-    loads[2].wait()
-    loads[3].wait()
 
     def halo_copies(k, src, which):
         copies = []
@@ -230,7 +278,7 @@
                 if i >= 4:
                     row = PLANE * (1 if STEPS[i][0] < 0 else 32) + (0 if STEPS[i][1] < 0 else 7)
                     stage_c[k, i - 4, pl.ds(c, 1), :] = src[c, pl.ds(row, 1), :]
-        for i, copy in halo_copies(k, src, which):
+        for i, copy in sorted(halo_copies(k, src, which), key=lambda item: ORDER.index(item[0])):
             @pl.when(there(STEPS[i]))
             def _(copy=copy):
                 copy.start()
@@ -257,18 +305,18 @@
             def _(copy=copy):
                 copy.wait_send()
 
-    def put(ref, rows, u):
+    def put(ref, vx, rows, u):
         ref[rows] = u
         vx[rows] = at_upper(u)
 
-    def place_halo(k, ref, which):
+    def place_halo(k, ref, vx, which):
         for c in range(3):
-            put(ref, (c, pl.ds(PLANE * 33, 8), slice(None)), land_y[k, 0, c])
+            put(ref, vx, (c, pl.ds(PLANE * 33, 8), slice(None)), land_y[k, 0, c])
             if 1 in which:
-                put(ref, (c, pl.ds(0, 8), slice(None)), land_y[k, 1, c])
+                put(ref, vx, (c, pl.ds(0, 8), slice(None)), land_y[k, 1, c])
             for j in range(4):
                 rows = (c, pl.ds(PLANE * (8 * j + 1) + 8, 8, PLANE), slice(None))
-                put(ref, rows, land_z[k, 0, c, pl.ds(8 * j, 8), :])
+                put(ref, vx, rows, land_z[k, 0, c, pl.ds(8 * j, 8), :])
                 if 3 in which:
                     u = land_z[k, 1, c, pl.ds(8 * j, 8), :]
                     low_z[c, pl.ds(8 * j + 1, 8), :] = u
@@ -291,14 +339,14 @@
         s0, d0, s1, d1 = u0 + x0, x0 - u0, u1 + x1, x1 - u1
         return {"00": s0 + s1, "01": d0 + d1, "10": s1 - s0, "11": d1 - d0}
 
-    def plane(ref, row):
+    def plane(ref, vx, row):
         row = pl.multiple_of(row, PLANE)
         return [
             pair_zx(ref[c, pl.ds(row, 8), :], vx[c, pl.ds(row, 8), :], ref[c, pl.ds(row + 1, 8), :], vx[c, pl.ds(row + 1, 8), :])
             for c in range(3)
         ]
 
-    def low_layer(ref):
+    def low_layer(ref, vx):
         for j in range(5):
             def rows(start):
                 return [
@@ -308,7 +356,7 @@
                     for c in range(3)
                 ]
             coefs = pair_y(rows(8 * j), rows(8 * j + 1))
-            for c, g in enumerate(stress(*coefs, mod_low[pl.ds(8 * j, 8), :])):
+            for c, g in enumerate(stress(*coefs, mod_z[pl.ds(8 * j + 1, 8), :])):
                 for part, start, pa, pb in zip(spread_y(g), (8 * j, 8 * j + 1), (p_low, p_up), (q_low, q_up)):
                     s, d = part["00"] + part["10"], part["01"] + part["11"]
                     pa[c, pl.ds(start, 8), :] = s - d
@@ -327,12 +375,12 @@
         keys = ("00", "01", "10", "11")
         return [dict(zip(keys, values[4 * c : 4 * c + 4])) for c in range(3)]
 
-    def forces(ref):
-        low, high = plane(ref, 0), plane(ref, PLANE)
+    def forces(ref, vx):
+        low, high = plane(ref, vx, 0), plane(ref, vx, PLANE)
         upper = [spread_y(g)[1] for g in stress(*pair_y(low, high), modulus(0))]
 
         def one(e, low, upper):
-            high = plane(ref, PLANE * (e + 1))
+            high = plane(ref, vx, PLANE * (e + 1))
             new = []
             for c, g in enumerate(stress(*pair_y(low, high), modulus(e))):
                 lo, hi = spread_y(g)
@@ -354,7 +402,7 @@
 
         lax.fori_loop(0, 8, body, flat(high) + flat(upper))
 
-    def finish(ref, image, after):
+    def finish(ref, image, after, after_x):
         def body(i, carry):
             for k in range(4):
                 y = 4 * i + k
@@ -368,12 +416,14 @@
                     image[c, y] = w
                     new = scale * w - SHIFT * v
                     after[c, pl.ds(row + PLANE, 8), :] = new
-                    vx[c, pl.ds(row + PLANE, 8), :] = at_upper(new)
+                    after_x[c, pl.ds(row + PLANE, 8), :] = at_upper(new)
             return carry
         lax.fori_loop(0, 8, body, 0)
 
     def dots(pairs):
         def get(ref, c, y):
+            if ref.shape[0] == 768:
+                return ref[pl.ds(pl.multiple_of(256 * c + 8 * y, 8), 8), :]
             if ref.shape[1] == FAR:
                 return ref[c, pl.ds(pl.multiple_of(PLANE * y + PLANE, PLANE), 8), :]
             return ref[c, y]
@@ -394,83 +444,141 @@
         for (slot, a, b), t in zip(pairs, total):
             acc[pl.ds(slot, 1), :] = jnp.sum(t, axis=0, keepdims=True)
 
-    for c in range(3):
-        def body(i, carry, c=c):
-            for k in range(4):
-                y = 4 * i + k
-                r0[c, y] = jnp.where(fixed[y] != 0, 0.0, force[c, y])
-            return carry
-        lax.fori_loop(0, 8, body, 0)
     every = tuple(range(8))
     clear_halo(0, every)
-    clear_halo(1, every)
-    clear_halo(2, LOWERS)
+    clear_halo(1, LOWERS)
     acc[...] = jnp.zeros(acc.shape, F32)
 
-    for step, down, copy in mod_copies:
-        @pl.when(there(down))
-        def _(copy=copy):
-            copy.wait_recv()
-
+    for i in range(8):
+        @pl.when(jnp.logical_not(away(i)))
+        def _(i=i):
+            first_copies[i].wait_recv()
+
+    mod[pl.ds(0, 8), :] = seen_y[1, 4]
+
+    def row_of(u, k):
+        return u[k : k + 1]
+
+    low_low, up_low, low_up, up_up = seen_c[3], seen_c[1], seen_c[2], seen_c[0]
+    for row, z1, z2, z7, z8 in (
+        (0, row_of(low_low, 4), row_of(low_low, 3), row_of(seen_y[1, 3], 7), row_of(low_up, 3)),
+        (1, row_of(low_low, 6), row_of(low_low, 5), row_of(seen_y[1, 4], 7), row_of(low_up, 4)),
+        (34, row_of(up_low, 4), row_of(up_low, 3), row_of(seen_y[0, 3], 7), row_of(up_up, 3)),
+    ):
+        at = pl.ds(row, 1)
+        mod_z[at, :] = z1
+        sum_low[at, :] = z1 + z2
+        sum_high[at, :] = z7 + z8
     for j in range(4):
-        mod_low[pl.ds(8 * j + 1, 8), :] = mod_face[pl.ds(8 * j, 8), :]
-    mod_low[pl.ds(0, 1), :] = mod_edge[pl.ds(7, 1), :]
-    for j in range(4):
-        tmp[pl.ds(PLANE * 8 * j, 8, PLANE), :] = mod_low[pl.ds(8 * j, 8), :] + mod_low[pl.ds(8 * j + 1, 8), :]
-
-    def sum_moduli(i, carry):
+        rows, to = pl.ds(8 * j, 8), pl.ds(8 * j + 2, 8)
+        z1 = seen_z[1, 4, rows, :]
+        mod_z[to, :] = z1
+        sum_low[to, :] = z1 + seen_z[1, 3, rows, :]
+        sum_high[to, :] = first_z[1, 4, rows, :] + seen_z[0, 3, rows, :]
+    for c in range(3):
+        for row, low, high in ((0, low_low, low_up), (33, up_low, up_up)):
+            low_z[c, pl.ds(row, 1), :] = row_of(low, c)
+            high_z[c, pl.ds(row, 1), :] = row_of(high, c)
+        for j in range(4):
+            rows, to = pl.ds(8 * j, 8), pl.ds(8 * j + 1, 8)
+            low_z[c, to, :] = seen_z[1, c, rows, :]
+            high_z[c, to, :] = seen_z[0, c, rows, :]
+
+    def inverse_of(t):
+        return 1.0 / jnp.maximum((KE_DIAG / UNIT) * (t + from_lower(t)), DIAG_FLOOR)
+
+    for j in range(5):
+        rows, above = pl.ds(8 * j, 8), pl.ds(8 * j + 1, 8)
+        low_scale = inverse_of(sum_low[rows, :] + sum_low[above, :])
+        high_scale = inverse_of(sum_high[rows, :] + sum_high[above, :])
+        tmp[pl.ds(PLANE * 8 * j, 8, PLANE), :] = mod_z[rows, :] + mod_z[above, :]
+        for c in range(3):
+            u = low_scale * low_z[c, rows, :]
+            low_z[c, rows, :] = u
+            low_zx[c, rows, :] = at_upper(u)
+            put(v0, x0, (c, pl.ds(PLANE * 8 * j + 8, 8, PLANE), slice(None)), high_scale * high_z[c, rows, :])
+
+    def keep_sum(n, t):
+        row = PLANE * n if isinstance(n, int) else pl.multiple_of(PLANE * n, PLANE)
+        sums[n] = t
+        tmp[pl.ds(row + 1, 8), :] = t
+
+    def begin(n, loads_of):
+        row = PLANE * n if isinstance(n, int) else pl.multiple_of(PLANE * n, PLANE)
+        scale = inverse_of(sums[n] + tmp[pl.ds(row, 8), :])
+        for c in range(3):
+            put(v0, x0, (c, pl.ds(row, 8), slice(None)), scale * loads_of(c))
+        return scale
+
+    keep_sum(0, seen_y[1, 3] + seen_y[1, 4])
+    keep_sum(33, modulus(32) + seen_y[0, 3])
+
+    def sum_own(i, carry):
         for k in range(4):
             y = 4 * i + k
-            t = modulus(y) + modulus(y + 1)
-            sums[y] = t
-            tmp[pl.ds(pl.multiple_of(PLANE * y, PLANE) + 1, 8), :] = t
+            keep_sum(y + 1, modulus(y) + modulus(y + 1))
         return carry
-    lax.fori_loop(0, 8, sum_moduli, 0)
-
-    def start(i, carry):
+    lax.fori_loop(0, 8, sum_own, 0)
+    begin(0, lambda c: seen_y[1, c])
+    begin(33, lambda c: seen_y[0, c])
+
+    def begin_own(i, carry):
         for k in range(4):
             y = 4 * i + k
-            t = sums[y] + tmp[pl.ds(pl.multiple_of(PLANE * y, PLANE), 8), :]
-            t = t + from_lower(t)
-            scale = 1.0 / jnp.maximum((KE_DIAG / UNIT) * t, DIAG_FLOOR)
-            inv[y] = scale
-            row = pl.multiple_of(PLANE * y + PLANE, PLANE)
-            for c in range(3):
-                v = scale * r0[c, y]
-                v0[c, pl.ds(row, 8), :] = v
-                vx[c, pl.ds(row, 8), :] = at_upper(v)
+            inv[y] = begin(y + 1, lambda c: r0[pl.ds(pl.multiple_of(256 * c + 8 * y, 8), 8), :])
         return carry
-    lax.fori_loop(0, 8, start, 0)
-
-    send_halo(0, v0, every)
-    dots([(0, r0, v0)])
-    wait_halo(0, v0, every)
-    place_halo(0, v0, every)
-    low_layer(v0)
-    forces(v0)
-    finish(v0, w0, v1)
-    send_halo(1, v1, every)
-    dots([(1, r0, v1), (3, v0, w0), (4, v1, w0)])
-    wait_halo(1, v1, every)
-    place_halo(1, v1, every)
-    low_layer(v1)
-    forces(v1)
-    finish(v1, w1, v2)
-    send_halo(2, v2, LOWERS)
+    lax.fori_loop(0, 8, begin_own, 0)
+
+    low_layer(v0, x0)
+    forces(v0, x0)
+    finish(v0, w0, v1, x1)
+    send_halo(0, v1, every)
+    dots([(0, r0, v0), (1, r0, v1), (3, v0, w0), (4, v1, w0)])
+    wait_halo(0, v1, every)
+    place_halo(0, v1, x1, every)
+    low_layer(v1, x1)
+    forces(v1, x1)
+    finish(v1, w1, v2, x2)
+    send_halo(1, v2, LOWERS)
     dots([(2, r0, v2), (5, v2, w0), (6, v1, w1), (7, v2, w1)])
-    wait_halo(2, v2, LOWERS)
-    place_halo(2, v2, LOWERS)
-    wait_sent(0, v0, every)
-
-    def stored_energy(i, carry):
-        low, total = unflat(carry[:12]), carry[12]
-        for k in range(4):
-            e = 4 * i + 1 + k
-            high = plane(v2, PLANE * (e + 1))
-            total = total + modulus(e) * energy_of(pair_y(low, high))
-            low = high
-        return flat(low) + (total,)
-    total = lax.fori_loop(0, 8, stored_energy, flat(plane(v2, PLANE)) + (zeros,))[12]
+    solid_scale = (-3.0 * (1.0 - MIN_MODULUS) * UNIT) * solid_rows
+    for block in range(4):
+        row = solid_scale[block : block + 1]
+        for y in range(8 * block, 8 * block + 8):
+            d = dens[y]
+            weighted[y] = row * (d * d * d)
+    wait_halo(1, v2, LOWERS)
+    place_halo(1, v2, x2, LOWERS)
+
+    basis = ((v0, x0), (v1, x1), (v2, x2))
+
+    def element_forms(chosen, pairs, with_total):
+        def body(i, carry):
+            lows = [unflat(carry[12 * k : 12 * k + 12]) for k in range(len(chosen))]
+            for k in range(2):
+                y = 2 * i + k
+                highs = [plane(*basis[b], PLANE * (y + 2)) for b in chosen]
+                coefs = {b: pair_y(low, high) for b, low, high in zip(chosen, lows, highs)}
+                factor = weighted[y]
+                for a in sorted({a for a, _ in pairs}):
+                    pulled = stress(*coefs[a], 1.0)
+                    for slot, (p, q) in enumerate(FORMS):
+                        if (p, q) in pairs and p == a:
+                            e = dot_forms(coefs[q], pulled)
+                            forms[slot, y] = factor * e
+                            if with_total:
+                                carry = carry[:-1] + (carry[-1] + modulus(y + 1) * e,)
+                lows = highs
+            out = ()
+            for low in lows:
+                out = out + flat(low)
+            return out + (carry[12 * len(chosen) :] if with_total else ())
+        init = ()
+        for b in chosen:
+            init = init + flat(plane(*basis[b], PLANE))
+        return lax.fori_loop(0, 16, body, init + ((zeros,) if with_total else ()))
+
+    total = element_forms((2,), ((2, 2),), True)[-1]
     acc[pl.ds(8, 1), :] = jnp.sum(total, axis=0, keepdims=True)
 
     column = jnp.sum(acc[...], axis=1, keepdims=True)
@@ -480,12 +588,16 @@
     for k, (axis, me, n, slots) in enumerate((("gy", iy, ny, slots_y), ("gz", iz, nz, slots_z))):
         slots[me] = part
 
-        def send_sum(i, carry, k=k, axis=axis, me=me, n=n, slots=slots):
+        far_y = sorted(range(1, ny), key=lambda i: -min(i, ny - i))
+        for i in far_y if axis == "gy" else far_first:
             pltpu.make_async_remote_copy(
-                slots.at[me], slots.at[me], sum_send.at[k], sum_recv.at[k], device_id={axis: lax.rem(me + i, n)},
+                slots.at[me], slots.at[me], sum_send.at[k], sum_recv.at[k],
+                device_id={axis: lax.rem(me + i, n) if axis == "gy" else other_z(i)},
             ).start()
-            return carry
-        lax.fori_loop(1, n, send_sum, 0)
+        if k == 0:
+            element_forms((0, 1), ((0, 0), (0, 1), (1, 1)), False)
+        else:
+            element_forms((0, 1, 2), ((2, 0), (2, 1)), False)
         whole = slots.at[pl.ds(0, n - 1)]
         pltpu.make_async_copy(whole, whole, sum_recv.at[k]).wait()
         part = jnp.sum(slots[:, 0, :], axis=0, keepdims=True)
@@ -506,55 +618,39 @@
     c2 = y2 / d2
     c1 = y1 / d1 - l21 * c2
     c0 = b0 / g00 - l10 * c1 - l20 * c2
-    c0, c1, c2 = (jnp.broadcast_to(c, (8, 128)) for c in (c0, c1, c2))
-
-    def combine(yy, c, off):
-        rows = (c, pl.ds(pl.multiple_of(PLANE * yy, PLANE) + off, 8), slice(None))
-        u = c0 * v0[rows] + c1 * v1[rows] + c2 * v2[rows]
-        v0[rows] = u
-        vx[rows] = at_upper(u)
-        return u
+    wide = lambda c: jnp.broadcast_to(c, (8, 128))
+    factors = [wide(c) for c in (c0 * c0, 2.0 * c0 * c1, c1 * c1, 2.0 * c2 * c0, 2.0 * c2 * c1, c2 * c2)]
+    c0, c1, c2 = wide(c0), wide(c1), wide(c2)
+
+    def weigh(i, carry):
+        for k in range(4):
+            y = 4 * i + k
+            total = factors[0] * forms[0, y]
+            for slot in range(1, 6):
+                total = total + factors[slot] * forms[slot, y]
+            weighted[y] = total
+        return carry
+    lax.fori_loop(0, 8, weigh, 0)
+
+    for i in far_first:
+        to = other_z(i)
+        pltpu.make_async_remote_copy(
+            weighted.at[pl.ds(to * lines, lines)], line_w.at[:, mine, :],
+            line_send.at[1], line_recv.at[1], device_id={"gz": to},
+        ).start()
+    for i in range(lines):
+        line_w[i, mine, :] = weighted[iz * lines + i]
 
     def displace(i, carry):
         for k in range(4):
+            row = pl.multiple_of(PLANE * (4 * i + k + 1), PLANE)
             for c in range(3):
-                disp[c, 4 * i + k] = combine(4 * i + k + 1, c, 0)
-                combine(4 * i + k + 1, c, 8)
+                rows = (c, pl.ds(row, 8), slice(None))
+                disp[c, 4 * i + k] = c0 * v0[rows] + c1 * v1[rows] + c2 * v2[rows]
         return carry
     lax.fori_loop(0, 8, displace, 0)
-    for c in range(3):
-        combine(33, c, 0)
-        combine(33, c, 8)
     disp_copy = pltpu.make_async_copy(disp, disp_h, store_sem.at[0])
     disp_copy.start()
-
-    solid_scale = (-3.0 * (1.0 - MIN_MODULUS) * UNIT) * solid_rows
-
-    def sensitivities(block):
-        def body(i, carry):
-            low = unflat(carry)
-            for k in range(4):
-                y = 8 * block + 4 * i + k
-                high = plane(v0, PLANE * (y + 2))
-                d = dens[y]
-                weighted[y] = (solid_scale[block : block + 1] * (d * d * d)) * energy_of(pair_y(low, high))
-                low = high
-            return flat(low)
-        return body
-    carry = flat(plane(v0, PLANE))
-    for block in range(4):
-        carry = lax.fori_loop(0, 2, sensitivities(block), carry)
-
-    def send_weighted(i, carry):
-        to = lax.rem(iz + i, nz)
-        pltpu.make_async_remote_copy(
-            weighted.at[pl.ds(to * lines, lines)], line_w.at[:, pl.ds(pl.multiple_of(iz * 8, 8), 8), :],
-            line_send.at[1], line_recv.at[1], device_id={"gz": to},
-        ).start()
-        return carry
-    lax.fori_loop(1, nz, send_weighted, 0)
-    for i in range(lines):
-        line_w[i, pl.ds(pl.multiple_of(iz * 8, 8), 8), :] = weighted[iz * lines + i]
 
     others = [ref.at[:, pl.ds(0, 8 * (nz - 1)), :] for ref in (line_d, line_w)]
     for k in range(2):
@@ -570,12 +666,12 @@
     for k, (n, slots) in enumerate(((ny, slots_y), (nz, slots_z))):
         whole = slots.at[pl.ds(0, n - 1)]
         pltpu.make_async_copy(whole, whole, sum_send.at[k]).wait()
-    for step, down, copy in mod_copies:
-        @pl.when(there(step))
-        def _(copy=copy):
-            copy.wait_send()
-    wait_sent(1, v1, every)
-    wait_sent(2, v2, LOWERS)
+    for i in range(8):
+        @pl.when(there(STEPS[i]))
+        def _(i=i):
+            first_copies[i].wait_send()
+    wait_sent(0, v1, every)
+    wait_sent(1, v2, LOWERS)
     disp_copy.wait()
     filt_copy.wait()
 
@@ -598,23 +694,25 @@
                 jax.ShapeDtypeStruct((3, 32, 8, 128), F32),
                 jax.ShapeDtypeStruct((lines, length, 128), F32),
             ),
-            in_specs=[pl.BlockSpec(memory_space=pl.ANY)] * 7,
-            out_specs=(pl.BlockSpec(memory_space=pl.ANY),) * 2,
+            in_specs=[pl.BlockSpec(memory_space=pltpu.HBM)] * 7,
+            out_specs=(pl.BlockSpec(memory_space=pltpu.HBM),) * 2,
             scratch_shapes=[
                 vmem(3, 32, 8, 128), vmem(32, 8, 128), pltpu.VMEM((4, 1, 16), jnp.int32), pltpu.VMEM((32, 8, 128), jnp.int32),
                 vmem(1, length), vmem(length, length), vmem(length, length),
-                vmem(264, 128), vmem(48, 128), vmem(32, 128), vmem(32, 128), vmem(8, 128),
-                vmem(32, 8, 128), vmem(3, 32, 8, 128), vmem(3, 32, 8, 128), vmem(3, 32, 8, 128),
-                *(node * 4), vmem(3, 48, 128), vmem(3, 48, 128),
-                vmem(3, 32, 8, 128), vmem(3, 32, 8, 128), vmem(3, 512, 128), vmem(3, 512, 128),
+                vmem(264, 128), vmem(48, 128), vmem(48, 128), vmem(48, 128), vmem(3, 48, 128),
+                vmem(32, 8, 128), vmem(768, 128), vmem(3, 32, 8, 128), vmem(3, 32, 8, 128),
+                *(node * 6), vmem(3, 48, 128), vmem(3, 48, 128),
+                vmem(3, 32, 8, 128), vmem(3, 32, 8, 128), vmem(3, 640, 128), vmem(3, 640, 128),
                 vmem(3, 48, 128), vmem(3, 48, 128), vmem(3, 48, 128), vmem(3, 48, 128),
-                vmem(3, 2, 3, 32, 128), vmem(3, 4, 8, 128), vmem(3, 2, 3, 8, 128), vmem(3, 2, 3, 32, 128), vmem(3, 4, 8, 128),
-                vmem(512, 128), vmem(32, 8, 128), vmem(16, 128), vmem(ny, 1, 128), vmem(nz, 1, 128),
+                vmem(2, 5, 8, 128), vmem(2, 5, 32, 128), vmem(4, 8, 128),
+                vmem(2, 5, 8, 128), vmem(2, 5, 32, 128), vmem(4, 8, 128),
+                vmem(2, 2, 3, 32, 128), vmem(2, 4, 8, 128), vmem(2, 2, 3, 8, 128), vmem(2, 2, 3, 32, 128), vmem(2, 4, 8, 128),
+                vmem(FAR, 128), vmem(34, 8, 128), vmem(16, 128), vmem(ny, 1, 128), vmem(nz, 1, 128), vmem(6, 32, 8, 128),
                 vmem(length, length), vmem(32, 8, 128), vmem(lines, length, 128), vmem(lines, length, 128),
                 vmem(3, 32, 8, 128), vmem(lines, length, 128),
-                dma(7), dma(2), dma(3), dma(3), dma(3, 8), dma(3, 8), dma(2), dma(2), dma(2), dma(2),
+                dma(7), dma(2), dma(8), dma(8), dma(2, 8), dma(2, 8), dma(2), dma(2), dma(2), dma(2),
             ],
-            compiler_params=pltpu.CompilerParams(collective_id=0, has_side_effects=True, vmem_limit_bytes=40 * 1024 * 1024),
+            compiler_params=pltpu.CompilerParams(collective_id=0, has_side_effects=True, vmem_limit_bytes=62 * 1024 * 1024),
             cost_estimate=pl.CostEstimate(flops=60_000_000, bytes_accessed=2_000_000, transcendentals=0),
         )(force, density, solid_blocks, fixed_nodes, filter_gain[None, :], jnp.asarray(cosine), jnp.asarray(sine))
 

time: 66 us -> 57 us (0.86)
  local copies, waits for them, and re-layouts: 7.46 us -> 2.46 us
  Pallas kernels: 57.6 us -> 53.5 us
    unnamed x16 -> x4, local copies, waits for them, and re-layouts: 7.46 us -> 2.46 us
    pallas_call x1, Pallas kernels: 57.6 us -> 53.5 us  [local(): pl.pallas_call(functools.partial(kernel, ny, nz, lines), out_shape=(jax.S...]
where the time goes in v2:
time: 57 us; the launch traced here: 56.6 us
  Pallas kernels  53.5 us (94%)
  local copies, waits for them, and re-layouts  2.46 us (4%)
  between operations  0.65 us (1%)
    pallas_call x1, Pallas kernels, local(): pl.pallas_call(functools.partial(kernel, ny, nz, lines), out_shape=(jax.S...  53.5 us
    unnamed x4, local copies, waits for them, and re-layouts  2.46 us

profile of v2, /device:TPU:6, one launch (start us, length us, event | category | flops | bytes accessed | tf_op | source)
XLA Modules:
  0.0 56.6 jit_solution(8528265986558428133)
XLA Ops:
  0.6 53.5 %shard_map.86 = (f32[3,32,8,128]{3,2,1,0:T(8,128)}, f32[1,256,128]{2,1,0:T(8,128)}) custom-call(f32[3,32,8,128]{3,2,1,0:T(8,128)} %force_h.1, f32[32,8,128]{2,1,0:T(8,128)} %dens_h.1, s32[4,1,16]{2,1,0:T(1,128)} %solid_h.1, s32[32,8,128]{2,1,0:T(8,128)} %fixed_h.1, f32[1,256]{1,0:T(1,128)} %bitcast.1, f32[256,256]{1,0:T(8,128)} %constant.4.clone.cos_h, ...), custom_call_target="tpu_custom_call" | custom-call | flops 60000000 | bytes 2000000 | tf_op jit(solution)/shard_map/pallas_call | solution.py:691
  54.1 0.0 copy-start
  54.1 1.8 %copy.11 = f32[3,32,8,128]{3,2,1,0:T(8,128)} copy(f32[3,32,8,128]{3,2,1,0:T(8,128)} %get-tuple-element.4) | data formatting | bytes 786432
  55.9 0.0 copy-done
  55.9 0.7 %copy.12 = f32[1,256,128]{2,1,0:T(8,128)} copy(f32[1,256,128]{2,1,0:T(8,128)S(1)} %copy-done) | data formatting | bytes 262144
Async XLA Ops:
  54.1 1.8 %copy-start = (f32[1,256,128]{2,1,0:T(8,128)S(1)}, f32[1,256,128]{2,1,0:T(8,128)}, u32[]{:S(2)}) copy-start(f32[1,256,128]{2,1,0:T(8,128)} %get-tuple-element.5) | copy-start | bytes 393220

commit v3 on v2

--- a/solution.py
+++ b/solution.py
@@ -100,7 +100,7 @@
     stage_z, stage_c, land_y, land_z, land_c,
     tmp, sums, acc, slots_y, slots_z, forms,
     circ, weighted, line_w, line_d, disp, filt,
-    load_sem, store_sem, first_send, first_recv, halo_send, halo_recv, sum_send, sum_recv, line_send, line_recv,
+    load_sem, store_sem, first_send, first_recv, halo_send, halo_recv, sum_send, sum_recv, line_send, line_recv, greet_sem,
 ):
     iy, iz = lax.axis_index("gy"), lax.axis_index("gz")
     lane = lax.broadcasted_iota(jnp.int32, (8, 128), 1)
@@ -133,16 +133,18 @@
     for sy, sz in STEPS:
         pl.semaphore_signal(barrier, 1, device_id=ring(sy, sz))
 
-    def greet_z(i, carry):
-        pl.semaphore_signal(barrier, 1, device_id={"gz": lax.rem(iz + i, nz)})
-        return carry
-
-    def greet_y(i, carry):
-        pl.semaphore_signal(barrier, 1, device_id={"gy": lax.rem(iy + i, ny)})
-        return carry
-
-    lax.fori_loop(2, nz - 1, greet_z, 0)
-    lax.fori_loop(2, ny - 1, greet_y, 0)
+    def greeters(r):
+        return [(a, axis, n) for a, (axis, n) in enumerate((("gy", ny), ("gz", nz))) if n >= 4 << r]
+
+    def greet(r):
+        for a, axis, n in greeters(r):
+            for d in (1 << r, n - (1 << r)):
+                to = lax.rem((iy if axis == "gy" else iz) + d, n)
+                pl.semaphore_signal(greet_sem.at[a, r], 1, device_id={axis: to})
+
+    def greeted(r):
+        for a, axis, n in greeters(r):
+            pl.semaphore_wait(greet_sem.at[a, r], 2)
 
     def there(step):
         sy, sz = step
@@ -198,7 +200,7 @@
         for k, (y, z) in enumerate(spots):
             first_c[i, pl.ds(3 + k, 1), :] = mod[pl.ds(8 * (y + 1) + z, 1), :]
 
-    pl.semaphore_wait(barrier, 8 + max(nz - 3, 0) + max(ny - 3, 0))
+    pl.semaphore_wait(barrier, 8)
 
     def part_of(arrays, i):
         return arrays[0].at[i] if i < 2 else arrays[1].at[i - 2] if i < 4 else arrays[2].at[i - 4]
@@ -215,6 +217,7 @@
         @pl.when(there(STEPS[i]))
         def _(i=i):
             first_copies[i].start()
+    greet(0)
 
     def away(i):
         return jnp.logical_not(there((-STEPS[i][0], -STEPS[i][1])))
@@ -238,12 +241,6 @@
 
     far_first = sorted(range(1, nz), key=hops)
     mine = pl.ds(pl.multiple_of(iz * 8, 8), 8)
-    for i in far_first:
-        to = other_z(i)
-        pltpu.make_async_remote_copy(
-            dens.at[pl.ds(to * lines, lines)], line_d.at[:, mine, :],
-            line_send.at[0], line_recv.at[0], device_id={"gz": to},
-        ).start()
     for i in range(lines):
         line_d[i, mine, :] = dens[iz * lines + i]
 
@@ -453,6 +450,8 @@
         @pl.when(jnp.logical_not(away(i)))
         def _(i=i):
             first_copies[i].wait_recv()
+    greeted(0)
+    greet(1)
 
     mod[pl.ds(0, 8), :] = seen_y[1, 4]
 
@@ -535,6 +534,8 @@
     send_halo(0, v1, every)
     dots([(0, r0, v0), (1, r0, v1), (3, v0, w0), (4, v1, w0)])
     wait_halo(0, v1, every)
+    greeted(1)
+    greet(2)
     place_halo(0, v1, x1, every)
     low_layer(v1, x1)
     forces(v1, x1)
@@ -548,6 +549,8 @@
             d = dens[y]
             weighted[y] = row * (d * d * d)
     wait_halo(1, v2, LOWERS)
+    greeted(2)
+    greet(3)
     place_halo(1, v2, x2, LOWERS)
 
     basis = ((v0, x0), (v1, x1), (v2, x2))
@@ -588,6 +591,8 @@
     for k, (axis, me, n, slots) in enumerate((("gy", iy, ny, slots_y), ("gz", iz, nz, slots_z))):
         slots[me] = part
 
+        if k == 1:
+            greeted(3)
         far_y = sorted(range(1, ny), key=lambda i: -min(i, ny - i))
         for i in far_y if axis == "gy" else far_first:
             pltpu.make_async_remote_copy(
@@ -597,6 +602,12 @@
         if k == 0:
             element_forms((0, 1), ((0, 0), (0, 1), (1, 1)), False)
         else:
+            for i in far_first:
+                to = other_z(i)
+                pltpu.make_async_remote_copy(
+                    dens.at[pl.ds(to * lines, lines)], line_d.at[:, mine, :],
+                    line_send.at[0], line_recv.at[0], device_id={"gz": to},
+                ).start()
             element_forms((0, 1, 2), ((2, 0), (2, 1)), False)
         whole = slots.at[pl.ds(0, n - 1)]
         pltpu.make_async_copy(whole, whole, sum_recv.at[k]).wait()
@@ -676,6 +687,19 @@
     filt_copy.wait()
 
 
+def settle(disp_h, filt_h, disp_o, filt_o, disp, filt, load_sem, store_sem):
+    parts = [(disp_h.at[c], disp.at[c], disp_o.at[c]) for c in range(3)] + [(filt_h, filt, filt_o)]
+    loads = [pltpu.make_async_copy(src, mid, load_sem.at[i]) for i, (src, mid, _) in enumerate(parts)]
+    stores = [pltpu.make_async_copy(mid, dst, store_sem.at[i]) for i, (_, mid, dst) in enumerate(parts)]
+    for load in loads:
+        load.start()
+    for load, store in zip(loads, stores):
+        load.wait()
+        store.start()
+    for store in stores:
+        store.wait()
+
+
 def solution(mesh):
     ny, nz = mesh.shape["gy"], mesh.shape["gz"]
     lines = 32 // nz
@@ -688,7 +712,7 @@
         vmem = lambda *shape: pltpu.VMEM(shape, F32)
         dma = lambda *shape: pltpu.SemaphoreType.DMA(shape)
         node = [vmem(3, FAR, 128)]
-        return pl.pallas_call(
+        outs = pl.pallas_call(
             functools.partial(kernel, ny, nz, lines),
             out_shape=(
                 jax.ShapeDtypeStruct((3, 32, 8, 128), F32),
@@ -711,10 +735,19 @@
                 vmem(length, length), vmem(32, 8, 128), vmem(lines, length, 128), vmem(lines, length, 128),
                 vmem(3, 32, 8, 128), vmem(lines, length, 128),
                 dma(7), dma(2), dma(8), dma(8), dma(2, 8), dma(2, 8), dma(2), dma(2), dma(2), dma(2),
+                pltpu.SemaphoreType.REGULAR((2, 4)),
             ],
             compiler_params=pltpu.CompilerParams(collective_id=0, has_side_effects=True, vmem_limit_bytes=62 * 1024 * 1024),
             cost_estimate=pl.CostEstimate(flops=60_000_000, bytes_accessed=2_000_000, transcendentals=0),
         )(force, density, solid_blocks, fixed_nodes, filter_gain[None, :], jnp.asarray(cosine), jnp.asarray(sine))
+        return pl.pallas_call(
+            settle,
+            out_shape=tuple(jax.ShapeDtypeStruct(x.shape, F32) for x in outs),
+            in_specs=[pl.BlockSpec(memory_space=pltpu.HBM)] * 2,
+            out_specs=(pl.BlockSpec(memory_space=pltpu.HBM),) * 2,
+            scratch_shapes=[vmem(3, 32, 8, 128), vmem(lines, length, 128), dma(4), dma(4)],
+            compiler_params=pltpu.CompilerParams(vmem_limit_bytes=62 * 1024 * 1024),
+        )(*outs)
 
     in_specs = (P(None, "gy", "gz", None), P("gy", "gz", None), P("gy", "gz", None), P("gy", "gz", None), P())
     out_specs = (P(None, "gy", "gz", None), P(("gy", "gz"), None, None))

time: 57 us -> 54.3 us (0.953)
  local copies, waits for them, and re-layouts: 2.46 us -> 0 us
    unnamed x4 -> x0, local copies, waits for them, and re-layouts: 2.46 us -> none
    pallas_call x0 -> x1, Pallas kernels: none -> 1.82 us  [local(): pl.pallas_call(settle, out_shape=tuple((jax.ShapeDtypeStruct(x.shape, F32...]
    pallas_call x1, Pallas kernels: 53.5 us -> 51.7 us  [local(): pl.pallas_call(functools.partial(kernel, ny, nz, lines), out_shape=(jax.S...]
where the time goes in v3:
time: 54.3 us; the launch traced here: 54.2 us
  Pallas kernels  53.5 us (99%)
  between operations  0.64 us (1%)
    pallas_call x1, Pallas kernels, local(): pl.pallas_call(functools.partial(kernel, ny, nz, lines), out_shape=(jax.S...  51.7 us
    pallas_call x1, Pallas kernels, local(): pl.pallas_call(settle, out_shape=tuple((jax.ShapeDtypeStruct(x.shape, F32...  1.82 us

profile of v3, /device:TPU:6, one launch (start us, length us, event | category | flops | bytes accessed | tf_op | source)
XLA Modules:
  0.0 54.2 jit_solution(16197199795548272410)
XLA Ops:
  0.6 51.7 %shard_map.86 = (f32[3,32,8,128]{3,2,1,0:T(8,128)}, f32[1,256,128]{2,1,0:T(8,128)}) custom-call(f32[3,32,8,128]{3,2,1,0:T(8,128)} %force_h.1, f32[32,8,128]{2,1,0:T(8,128)} %dens_h.1, s32[4,1,16]{2,1,0:T(1,128)} %solid_h.1, s32[32,8,128]{2,1,0:T(8,128)} %fixed_h.1, f32[1,256]{1,0:T(1,128)} %bitcast.1, f32[256,256]{1,0:T(8,128)} %constant.4.clone.cos_h, ...), custom_call_target="tpu_custom_call" | custom-call | flops 60000000 | bytes 2000000 | tf_op jit(solution)/shard_map/pallas_call | solution.py:715
  52.3 1.8 %shard_map.87 = (f32[3,32,8,128]{3,2,1,0:T(8,128)}, f32[1,256,128]{2,1,0:T(8,128)}) custom-call(f32[3,32,8,128]{3,2,1,0:T(8,128)} %get-tuple-element.4.disp_h, f32[1,256,128]{2,1,0:T(8,128)} %get-tuple-element.5.filt_h), custom_call_target="tpu_custom_call" | custom-call | tf_op jit(solution)/shard_map/pallas_call | solution.py:743

commit v4 on v3

--- a/solution.py
+++ b/solution.py
@@ -401,8 +401,8 @@
 
     def finish(ref, image, after, after_x):
         def body(i, carry):
-            for k in range(4):
-                y = 4 * i + k
+            for k in range(16):
+                y = 16 * i + k
                 held = fixed[y] != 0
                 scale = inv[y]
                 row = pl.multiple_of(PLANE * y, PLANE)
@@ -415,7 +415,7 @@
                     after[c, pl.ds(row + PLANE, 8), :] = new
                     after_x[c, pl.ds(row + PLANE, 8), :] = at_upper(new)
             return carry
-        lax.fori_loop(0, 8, body, 0)
+        lax.fori_loop(0, 2, body, 0)
 
     def dots(pairs):
         def get(ref, c, y):
@@ -522,11 +522,11 @@
     begin(33, lambda c: seen_y[0, c])
 
     def begin_own(i, carry):
-        for k in range(4):
-            y = 4 * i + k
+        for k in range(8):
+            y = 8 * i + k
             inv[y] = begin(y + 1, lambda c: r0[pl.ds(pl.multiple_of(256 * c + 8 * y, 8), 8), :])
         return carry
-    lax.fori_loop(0, 8, begin_own, 0)
+    lax.fori_loop(0, 4, begin_own, 0)
 
     low_layer(v0, x0)
     forces(v0, x0)

time: 54.3 us -> 52.1 us (0.959)
  Pallas kernels: 53.5 us -> 51.2 us
    pallas_call x1, Pallas kernels: 51.7 us -> 49.4 us  [local(): pl.pallas_call(functools.partial(kernel, ny, nz, lines), out_shape=(jax.S...]
where the time goes in v4:
time: 52.1 us; the launch traced here: 51.9 us
  Pallas kernels  51.2 us (98%)
  between operations  0.64 us (1%)
    pallas_call x1, Pallas kernels, local(): pl.pallas_call(functools.partial(kernel, ny, nz, lines), out_shape=(jax.S...  49.4 us
    pallas_call x1, Pallas kernels, local(): pl.pallas_call(settle, out_shape=tuple((jax.ShapeDtypeStruct(x.shape, F32...  1.82 us

profile of v4, /device:TPU:6, one launch (start us, length us, event | category | flops | bytes accessed | tf_op | source)
XLA Modules:
  0.0 51.9 jit_solution(14480019407193285854)
XLA Ops:
  0.6 49.4 %shard_map.86 = (f32[3,32,8,128]{3,2,1,0:T(8,128)}, f32[1,256,128]{2,1,0:T(8,128)}) custom-call(f32[3,32,8,128]{3,2,1,0:T(8,128)} %force_h.1, f32[32,8,128]{2,1,0:T(8,128)} %dens_h.1, s32[4,1,16]{2,1,0:T(1,128)} %solid_h.1, s32[32,8,128]{2,1,0:T(8,128)} %fixed_h.1, f32[1,256]{1,0:T(1,128)} %bitcast.1, f32[256,256]{1,0:T(8,128)} %constant.4.clone.cos_h, ...), custom_call_target="tpu_custom_call" | custom-call | flops 60000000 | bytes 2000000 | tf_op jit(solution)/shard_map/pallas_call | solution.py:715
  50.1 1.8 %shard_map.87 = (f32[3,32,8,128]{3,2,1,0:T(8,128)}, f32[1,256,128]{2,1,0:T(8,128)}) custom-call(f32[3,32,8,128]{3,2,1,0:T(8,128)} %get-tuple-element.4.disp_h, f32[1,256,128]{2,1,0:T(8,128)} %get-tuple-element.5.filt_h), custom_call_target="tpu_custom_call" | custom-call | tf_op jit(solution)/shard_map/pallas_call | solution.py:743
